TPU v7x, 512 devices: a whole 4x8x8 slice. The times are simulated.
512 devices in a mesh: dp: 16 (over z, core), ctx: 32 (over x, y).
Axes of the slice: x: 4, y: 8, z: 8, core: 2. Of those that a mesh axis runs over, the one named last changes fastest.
Arguments:
- query_rows: bfloat16 [131072, 2048], P(('dp', 'ctx')), parts along dimension 0, may hold values from -64 to 64
- key_rows: bfloat16 [131072, 512], P(('dp', 'ctx')), parts along dimension 0, may hold values from -32 to 32
- value_rows: bfloat16 [131072, 512], P(('dp', 'ctx')), parts along dimension 0, may hold values from -6 to 6
- doc_lengths: int32 [288], P('dp'), parts along dimension 0, may hold values from 1 to 1793, 8192 in all
- row_owner: int32 [131072, 1], P(('dp', 'ctx')), parts along dimension 0, may hold values from 0 to 31; in each aligned block of 256 rows (0 to 255, 256 to 511, ...) at most 16 rows name the same one
Outputs:
- shard_rows: bfloat16 [262144, 2048], P(('dp', 'ctx')), parts along dimension 0
There are 16 independent parts, one for each index of `dp`. A program takes and returns all parts, laid end to end along the dimension named above; each array names one. Nothing has to cross between parts.
Inputs may be any that keep to these rules, and one draw needn't show every extreme that they name: `doc_lengths`: the lengths sum to 8192; the largest is 1793. `row_owner`: among the rows of one shard at most 16 name the same owner, and in every draw some shard's rows name one owner exactly 16 times.
All inputs are finite; a program needn't handle non-finite values.
Results may differ from a plain program's by a relative error of at most 0.0036.
Values may be sent and summed in bfloat16 or wider, within the bound.
No kernel may reach another device: no remote copies, remote signals or barrier semaphores. Data moves between devices by JAX's collectives and lax.ppermute only.
A program may use at most 64 MiB of HBM per device.

v0:
```python
import math

import jax
import jax.numpy as jnp
from jax import lax
from jax.sharding import PartitionSpec as P

H = 16
KVH = 4
HD = 128
SPAN = 8


def from_behind(value, axis, steps):
    count = lax.axis_size(axis)
    initial, last = (max(0, -steps), min(count, count - steps))
    return lax.ppermute(value, axis, [(source, source + steps) for source in range(initial, last)])


def segment_of(positions, doc_lengths):
    doc_ends = jnp.cumsum(doc_lengths)
    return jnp.sum((doc_ends[None, :] <= positions[:, None]).astype(jnp.int32), axis=1)


def on_device(query_rows, key_rows, value_rows, doc_lengths, row_owner):
    row_count = query_rows.shape[0]
    devices = lax.axis_size("ctx")
    shard_index = lax.axis_index("ctx")
    pair_slots = 2 * row_count // devices
    features = query_rows.shape[1]
    stacked = jnp.stack([key_rows, value_rows])
    pieces = []
    for offset in range(SPAN - 1, 0, -1):
        pieces.append(from_behind(stacked, "ctx", offset))
    pieces.append(stacked)
    window = jnp.concatenate(pieces, axis=1)
    key_window = window[0]
    value_window = window[1]
    start = shard_index * row_count
    query_pos = start + jnp.arange(row_count, dtype=jnp.int32)
    key_pos = start - (SPAN - 1) * row_count + jnp.arange(SPAN * row_count, dtype=jnp.int32)
    query_seg = segment_of(query_pos, doc_lengths)
    key_seg = segment_of(key_pos, doc_lengths)
    visible = (
        (query_seg[:, None] == key_seg[None, :])
        & (key_pos[None, :] <= query_pos[:, None])
        & (key_pos[None, :] >= 0)
    )
    mask = visible[:, None, :]
    group_size = H // KVH
    outputs = []
    for head_group in range(KVH):
        query_part = query_rows[
            :, head_group * group_size * HD : (head_group + 1) * group_size * HD
        ].reshape(row_count, group_size, HD)
        key_part = key_window[:, head_group * HD : (head_group + 1) * HD]
        value_part = value_window[:, head_group * HD : (head_group + 1) * HD]
        scores = jnp.einsum(
            "qgd,nd->qgn", query_part, key_part, preferred_element_type=jnp.float32
        ) * (1.0 / math.sqrt(HD))
        scores = jnp.where(mask, scores, -jnp.inf)
        row_max = jnp.max(scores, axis=2, keepdims=True)
        expo = jnp.where(mask, jnp.exp(scores - row_max), 0.0)
        denominator = jnp.sum(expo, axis=2)
        weights = expo.astype(jnp.bfloat16)
        weighted = jnp.einsum(
            "qgn,nd->qgd", weights, value_part, preferred_element_type=jnp.float32
        )
        attended = (weighted / denominator[..., None]).astype(jnp.bfloat16)
        outputs.append(attended.reshape(row_count, group_size * HD))
    out_rows = jnp.concatenate(outputs, axis=1)
    owners = row_owner[:, 0]
    onehot = (owners[:, None] == jnp.arange(devices, dtype=jnp.int32)[None, :]).astype(jnp.int32)
    running = jnp.cumsum(onehot, axis=0)
    slot_rank = jnp.sum(onehot * (running - 1), axis=1)
    send_slot = owners * pair_slots + slot_rank
    outgoing = jnp.zeros((devices * pair_slots, features), jnp.bfloat16).at[send_slot].set(out_rows)
    received = lax.all_to_all(
        outgoing.reshape(devices, pair_slots, features),
        "ctx",
        split_axis=0,
        concat_axis=0,
        tiled=True,
    )
    return received.reshape(devices * pair_slots, features)


def solution(mesh):
    in_specs = (
        P(("dp", "ctx"), None),
        P(("dp", "ctx"), None),
        P(("dp", "ctx"), None),
        P("dp"),
        P(("dp", "ctx"), None),
    )
    out_specs = P(("dp", "ctx"), None)
    return jax.shard_map(
        on_device, mesh=mesh, in_specs=in_specs, out_specs=out_specs, check_vma=False
    )
```

profile of v0, /device:TPU:456, one launch (start us, length us, event | category | flops | bytes accessed | tf_op | source)
XLA Modules:
  0.0 225.2 jit_solution(28337601251277327)
XLA Ops:
  0.0 1.1 pad_maximum_fusion
  1.1 4.1 %collective-permute-start = (bf16[2,256,512]{2,1,0:T(8,128)(2,1)S(1)}, bf16[2,256,512]{2,1,0:T(8,128)(2,1)}, u32[]{:S(2)}, u32[]{:S(2)}) collective-permute-start(bf16[2,256,512]{2,1,0:T(8,128)(2,1)S(1)} %pad_maximum_fusion), channel_id=1, source_target_pairs={{0,7},{1,8},{2,9},{3,10},{4,11},{5,12},{6,13},{7,14},{8,15},{9,16}... | collective-permute-start | bytes 1572872 | tf_op jit(solution)/shard_map/ppermute | solution.py:17
  5.2 6.2 %collective-permute-start.1 = (bf16[2,256,512]{2,1,0:T(8,128)(2,1)S(1)}, bf16[2,256,512]{2,1,0:T(8,128)(2,1)}, u32[]{:S(2)}, u32[]{:S(2)}) collective-permute-start(bf16[2,256,512]{2,1,0:T(8,128)(2,1)S(1)} %pad_maximum_fusion), channel_id=1, source_target_pairs={{0,6},{1,7},{2,8},{3,9},{4,10},{5,11},{6,12},{7,13},{8,14},{9,15},... | collective-permute-start | bytes 1572872 | tf_op jit(solution)/shard_map/ppermute | solution.py:17
  11.4 4.9 %collective-permute-start.2 = (bf16[2,256,512]{2,1,0:T(8,128)(2,1)S(1)}, bf16[2,256,512]{2,1,0:T(8,128)(2,1)}, u32[]{:S(2)}, u32[]{:S(2)}) collective-permute-start(bf16[2,256,512]{2,1,0:T(8,128)(2,1)S(1)} %pad_maximum_fusion), channel_id=1, source_target_pairs={{0,5},{1,6},{2,7},{3,8},{4,9},{5,10},{6,11},{7,12},{8,13},{9,14},{... | collective-permute-start | bytes 1572872 | tf_op jit(solution)/shard_map/ppermute | solution.py:17
  16.2 5.0 %collective-permute-start.3 = (bf16[2,256,512]{2,1,0:T(8,128)(2,1)S(1)}, bf16[2,256,512]{2,1,0:T(8,128)(2,1)}, u32[]{:S(2)}, u32[]{:S(2)}) collective-permute-start(bf16[2,256,512]{2,1,0:T(8,128)(2,1)S(1)} %pad_maximum_fusion), channel_id=1, source_target_pairs={{0,4},{1,5},{2,6},{3,7},{4,8},{5,9},{6,10},{7,11},{8,12},{9,13},{1... | collective-permute-start | bytes 1572872 | tf_op jit(solution)/shard_map/ppermute | solution.py:17
  21.3 3.6 %collective-permute-start.4 = (bf16[2,256,512]{2,1,0:T(8,128)(2,1)S(1)}, bf16[2,256,512]{2,1,0:T(8,128)(2,1)S(1)}, u32[]{:S(2)}, u32[]{:S(2)}) collective-permute-start(bf16[2,256,512]{2,1,0:T(8,128)(2,1)S(1)} %pad_maximum_fusion), channel_id=1, source_target_pairs={{0,3},{1,4},{2,5},{3,6},{4,7},{5,8},{6,9},{7,10},{8,11},{9,12},{10... | collective-permute-start | bytes 1572872 | tf_op jit(solution)/shard_map/ppermute | solution.py:17
  24.9 1.3 fusion.76
  27.3 2.6 %and_and_fusion = pred[256,2048]{0,1:T(8,128)(4,1)} fusion(s32[256]{0:T(256)S(1)} %iota_add_fusion.1, s32[256]{0:T(256)S(1)} %convert_reduce_fusion.1, s32[2048]{0:T(1024)S(1)} %iota_add_fusion, s32[2048]{0:T(1024)S(1)} %convert_reduce_fusion, pred[2048]{0:T(1024)(128)(4,1)S(1)} %broadcast_compare_fusion), kind=kLoop, calls=%fused_computation.39 | loop fusion | flops 2097152 | bytes 544768 | tf_op jit(solution)/shard_map/and | solution.py:45
  33.4 4.5 %collective-permute-start.5 = (bf16[2,256,512]{2,1,0:T(8,128)(2,1)S(1)}, bf16[2,256,512]{2,1,0:T(8,128)(2,1)S(1)}, u32[]{:S(2)}, u32[]{:S(2)}) collective-permute-start(bf16[2,256,512]{2,1,0:T(8,128)(2,1)S(1)} %pad_maximum_fusion), channel_id=1, source_target_pairs={{0,2},{1,3},{2,4},{3,5},{4,6},{5,7},{6,8},{7,9},{8,10},{9,11},{10,... | collective-permute-start | bytes 1572872 | tf_op jit(solution)/shard_map/ppermute | solution.py:17
  37.9 1.1 constant_dynamic-update-slice_fusion.7
  39.0 29.2 %collective-permute-start.6 = (bf16[2,256,512]{2,1,0:T(8,128)(2,1)S(1)}, bf16[2,256,512]{2,1,0:T(8,128)(2,1)S(1)}, u32[]{:S(2)}, u32[]{:S(2)}) collective-permute-start(bf16[2,256,512]{2,1,0:T(8,128)(2,1)S(1)} %pad_maximum_fusion), channel_id=1, source_target_pairs={{0,1},{1,2},{2,3},{3,4},{4,5},{5,6},{6,7},{7,8},{8,9},{9,10},{10,1... | collective-permute-start | bytes 1572872 | tf_op jit(solution)/shard_map/ppermute | solution.py:17
  68.3 1.1 constant_dynamic-update-slice_fusion.6
  69.3 1.1 constant_dynamic-update-slice_fusion.5
  70.4 5.9 %collective-permute-done.3 = bf16[2,256,512]{2,1,0:T(8,128)(2,1)} collective-permute-done((bf16[2,256,512]{2,1,0:T(8,128)(2,1)S(1)}, bf16[2,256,512]{2,1,0:T(8,128)(2,1)}, u32[]{:S(2)}, u32[]{:S(2)}) %collective-permute-start.3) | collective-permute-done | bytes 524320 | tf_op jit(solution)/shard_map/ppermute | solution.py:17
  77.5 22.0 %collective-permute-done.5 = bf16[2,256,512]{2,1,0:T(8,128)(2,1)S(1)} collective-permute-done((bf16[2,256,512]{2,1,0:T(8,128)(2,1)S(1)}, bf16[2,256,512]{2,1,0:T(8,128)(2,1)S(1)}, u32[]{:S(2)}, u32[]{:S(2)}) %collective-permute-start.5) | collective-permute-done | bytes 524320 | tf_op jit(solution)/shard_map/ppermute | solution.py:17
  99.5 15.5 %collective-permute-done.6 = bf16[2,256,512]{2,1,0:T(8,128)(2,1)S(1)} collective-permute-done((bf16[2,256,512]{2,1,0:T(8,128)(2,1)S(1)}, bf16[2,256,512]{2,1,0:T(8,128)(2,1)S(1)}, u32[]{:S(2)}, u32[]{:S(2)}) %collective-permute-start.6) | collective-permute-done | bytes 524320 | tf_op jit(solution)/shard_map/ppermute | solution.py:17
  115.1 1.6 slice_bitcast_fusion
  116.7 1.2 fusion.64
  117.9 6.0 %fusion.80 = (f32[256,4]{0,1:T(4,128)S(1)}, bf16[256,4,2048]{0,2,1:T(8,128)(2,1)}) fusion(f32[2048,256,4]{1,0,2:T(8,128)S(1)} %fusion.64, pred[256,2048]{0,1:T(8,128)(4,1)S(1)} %copy-done.2), kind=kOutput, calls=%fused_computation.104 | output fusion | flops 16779264 | bytes 13111296 | tf_op jit(solution)/shard_map/sub | solution.py:63
  124.0 3.1 %fusion.49 = bf16[256,4,128]{0,2,1:T(8,128)(2,1)S(1)} fusion(bf16[256,4,2048]{0,2,1:T(8,128)(2,1)} %get-tuple-element.18, bf16[2048,512]{1,0:T(8,128)(2,1)} %get-tuple-element.5, f32[256,4]{0,1:T(4,128)S(1)} %get-tuple-element.17), kind=kOutput, calls=%fused_computation.47 | convolution fusion | flops 537133056 | bytes 4984832 | tf_op jit(solution)/shard_map/qgn,nd->qgd/dot_general | solution.py:66
  127.2 1.2 fusion.63
  128.5 5.8 %fusion.79 = (f32[256,4]{0,1:T(4,128)S(1)}, bf16[256,4,2048]{0,2,1:T(8,128)(2,1)}) fusion(f32[2048,256,4]{1,0,2:T(8,128)S(1)} %fusion.63, pred[256,2048]{0,1:T(8,128)(4,1)S(1)} %copy-done.3), kind=kOutput, calls=%fused_computation.103 | output fusion | flops 16779264 | bytes 13111296 | tf_op jit(solution)/shard_map/sub | solution.py:63
  134.3 3.1 %fusion.46 = bf16[256,4,128]{0,2,1:T(8,128)(2,1)S(1)} fusion(bf16[256,4,2048]{0,2,1:T(8,128)(2,1)} %get-tuple-element.16, bf16[2048,512]{1,0:T(8,128)(2,1)} %get-tuple-element.5, f32[256,4]{0,1:T(4,128)S(1)} %get-tuple-element.15), kind=kOutput, calls=%fused_computation.46 | convolution fusion | flops 537133056 | bytes 4984832 | tf_op jit(solution)/shard_map/qgn,nd->qgd/dot_general | solution.py:66
  137.5 1.2 fusion.62
  138.8 5.8 %fusion.78 = (f32[256,4]{0,1:T(4,128)S(1)}, bf16[256,4,2048]{0,2,1:T(8,128)(2,1)}) fusion(f32[2048,256,4]{1,0,2:T(8,128)S(1)} %fusion.62, pred[256,2048]{0,1:T(8,128)(4,1)S(1)} %copy-done.4), kind=kOutput, calls=%fused_computation.102 | output fusion | flops 16779264 | bytes 13111296 | tf_op jit(solution)/shard_map/sub | solution.py:63
  144.6 3.1 %fusion.43 = bf16[256,4,128]{0,2,1:T(8,128)(2,1)S(1)} fusion(bf16[256,4,2048]{0,2,1:T(8,128)(2,1)} %get-tuple-element.14, bf16[2048,512]{1,0:T(8,128)(2,1)} %get-tuple-element.5, f32[256,4]{0,1:T(4,128)S(1)} %get-tuple-element.13), kind=kOutput, calls=%fused_computation.45 | convolution fusion | flops 537133056 | bytes 4984832 | tf_op jit(solution)/shard_map/qgn,nd->qgd/dot_general | solution.py:66
  147.9 1.2 fusion.61
  149.1 5.8 %fusion.77 = (f32[256,4]{0,1:T(4,128)S(1)}, bf16[256,4,2048]{0,2,1:T(8,128)(2,1)}) fusion(f32[2048,256,4]{1,0,2:T(8,128)S(1)} %fusion.61, pred[256,2048]{0,1:T(8,128)(4,1)S(1)} %copy-done.5), kind=kOutput, calls=%fused_computation.101 | output fusion | flops 16779264 | bytes 13111296 | tf_op jit(solution)/shard_map/sub | solution.py:63
  155.0 3.1 %fusion.40 = bf16[256,4,128]{0,2,1:T(8,128)(2,1)S(1)} fusion(bf16[256,4,2048]{0,2,1:T(8,128)(2,1)} %get-tuple-element.12, bf16[2048,512]{1,0:T(8,128)(2,1)} %get-tuple-element.5, f32[256,4]{0,1:T(4,128)S(1)} %get-tuple-element.11), kind=kOutput, calls=%fused_computation.44 | convolution fusion | flops 537133056 | bytes 4984832 | tf_op jit(solution)/shard_map/qgn,nd->qgd/dot_general | solution.py:66
  158.2 2.9 %scatter_custom_fusion = bf16[512,2048]{1,0:T(8,128)(2,1)S(1)} fusion(s32[256]{0:T(256)S(1)} %bitcast.129, bf16[256,512]{1,0:T(8,128)(2,1)S(1)} %copy.58, bf16[]{:T(256)} %constant.43, bf16[256,512]{1,0:T(8,128)(2,1)S(1)} %copy.57, bf16[256,512]{1,0:T(8,128)(2,1)S(1)} %copy.56, bf16[256,512]{1,0:T(8,128)(2,1)S(1)} %copy.55, bf16[]{:T(256)} %constant.11.clone.1), kind=kCustom, calls=%fused_computation.48 | custom fusion | flops 4194304 | bytes 3145732 | tf_op jit(solution)/shard_map/scatter | solution.py:77
  161.1 62.8 %all_to_all.5 = bf16[32,16,2048]{2,1,0:T(8,128)(2,1)S(1)} all-to-all(bf16[32,16,2048]{2,1,0:T(8,128)(2,1)S(1)} %bitcast.112), channel_id=1, replica_groups=mesh['dp'=16,'ctx'=32] {'ctx'}, dimensions={0} | all-to-all | bytes 4194304 | tf_op jit(solution)/shard_map/all_to_all | solution.py:78
  223.9 1.3 copy.89
  (44 shorter events, 6.4 us)
Async XLA Ops:
  1.1 32.3 %collective-permute-start = (bf16[2,256,512]{2,1,0:T(8,128)(2,1)S(1)}, bf16[2,256,512]{2,1,0:T(8,128)(2,1)}, u32[]{:S(2)}, u32[]{:S(2)}) collective-permute-start(bf16[2,256,512]{2,1,0:T(8,128)(2,1)S(1)} %pad_maximum_fusion), channel_id=1, source_target_pairs={{0,7},{1,8},{2,9},{3,10},{4,11},{5,12},{6,13},{7,14},{8,15},{9,16}... | collective-permute-start | bytes 1572872 | tf_op jit(solution)/shard_map/ppermute | solution.py:17
  5.2 33.8 %collective-permute-start.1 = (bf16[2,256,512]{2,1,0:T(8,128)(2,1)S(1)}, bf16[2,256,512]{2,1,0:T(8,128)(2,1)}, u32[]{:S(2)}, u32[]{:S(2)}) collective-permute-start(bf16[2,256,512]{2,1,0:T(8,128)(2,1)S(1)} %pad_maximum_fusion), channel_id=1, source_target_pairs={{0,6},{1,7},{2,8},{3,9},{4,10},{5,11},{6,12},{7,13},{8,14},{9,15},... | collective-permute-start | bytes 1572872 | tf_op jit(solution)/shard_map/ppermute | solution.py:17
  11.4 58.0 %collective-permute-start.2 = (bf16[2,256,512]{2,1,0:T(8,128)(2,1)S(1)}, bf16[2,256,512]{2,1,0:T(8,128)(2,1)}, u32[]{:S(2)}, u32[]{:S(2)}) collective-permute-start(bf16[2,256,512]{2,1,0:T(8,128)(2,1)S(1)} %pad_maximum_fusion), channel_id=1, source_target_pairs={{0,5},{1,6},{2,7},{3,8},{4,9},{5,10},{6,11},{7,12},{8,13},{9,14},{... | collective-permute-start | bytes 1572872 | tf_op jit(solution)/shard_map/ppermute | solution.py:17
  16.2 60.1 %collective-permute-start.3 = (bf16[2,256,512]{2,1,0:T(8,128)(2,1)S(1)}, bf16[2,256,512]{2,1,0:T(8,128)(2,1)}, u32[]{:S(2)}, u32[]{:S(2)}) collective-permute-start(bf16[2,256,512]{2,1,0:T(8,128)(2,1)S(1)} %pad_maximum_fusion), channel_id=1, source_target_pairs={{0,4},{1,5},{2,6},{3,7},{4,8},{5,9},{6,10},{7,11},{8,12},{9,13},{1... | collective-permute-start | bytes 1572872 | tf_op jit(solution)/shard_map/ppermute | solution.py:17
  21.3 56.1 %collective-permute-start.4 = (bf16[2,256,512]{2,1,0:T(8,128)(2,1)S(1)}, bf16[2,256,512]{2,1,0:T(8,128)(2,1)S(1)}, u32[]{:S(2)}, u32[]{:S(2)}) collective-permute-start(bf16[2,256,512]{2,1,0:T(8,128)(2,1)S(1)} %pad_maximum_fusion), channel_id=1, source_target_pairs={{0,3},{1,4},{2,5},{3,6},{4,7},{5,8},{6,9},{7,10},{8,11},{9,12},{10... | collective-permute-start | bytes 1572872 | tf_op jit(solution)/shard_map/ppermute | solution.py:17
  33.1 81.9 %copy-start = (bf16[256,512]{1,0:T(8,128)(2,1)S(1)}, bf16[256,512]{1,0:T(8,128)(2,1)}, u32[]{:S(2)}) copy-start(bf16[256,512]{1,0:T(8,128)(2,1)} %param.7) | copy-start | bytes 786436
  33.1 81.9 %copy-start.1 = (bf16[256,512]{1,0:T(8,128)(2,1)S(1)}, bf16[256,512]{1,0:T(8,128)(2,1)}, u32[]{:S(2)}) copy-start(bf16[256,512]{1,0:T(8,128)(2,1)} %param.6) | copy-start | bytes 786436
  33.4 66.0 %collective-permute-start.5 = (bf16[2,256,512]{2,1,0:T(8,128)(2,1)S(1)}, bf16[2,256,512]{2,1,0:T(8,128)(2,1)S(1)}, u32[]{:S(2)}, u32[]{:S(2)}) collective-permute-start(bf16[2,256,512]{2,1,0:T(8,128)(2,1)S(1)} %pad_maximum_fusion), channel_id=1, source_target_pairs={{0,2},{1,3},{2,4},{3,5},{4,6},{5,7},{6,8},{7,9},{8,10},{9,11},{10,... | collective-permute-start | bytes 1572872 | tf_op jit(solution)/shard_map/ppermute | solution.py:17
  39.0 76.0 %collective-permute-start.6 = (bf16[2,256,512]{2,1,0:T(8,128)(2,1)S(1)}, bf16[2,256,512]{2,1,0:T(8,128)(2,1)S(1)}, u32[]{:S(2)}, u32[]{:S(2)}) collective-permute-start(bf16[2,256,512]{2,1,0:T(8,128)(2,1)S(1)} %pad_maximum_fusion), channel_id=1, source_target_pairs={{0,1},{1,2},{2,3},{3,4},{4,5},{5,6},{6,7},{7,8},{8,9},{9,10},{10,1... | collective-permute-start | bytes 1572872 | tf_op jit(solution)/shard_map/ppermute | solution.py:17
  116.7 1.2 copy-start.2
  127.2 1.3 copy-start.3
  137.5 1.3 copy-start.4
  147.9 1.3 copy-start.5
where the time goes:
time: 226 us; the launch traced here: 225 us
  blocking collectives  62.8 us (28%)
  starting transfers between devices  57.5 us (25%)
  waiting for transfers between devices  43.4 us (19%)
  other arithmetic  33.3 us (15%)
  matrix products  17.3 us (8%)
  local copies, waits for them, and re-layouts  10.6 us (5%)
    all_to_all x1, blocking collectives, on_device(): lax.all_to_all(outgoing.reshape(devices, pair_slots, features), 'ctx', sp...  62.8 us
    ppermute x7, starting transfers between devices, from_behind(): lax.ppermute(value, axis, [(source, source + steps) for source in range(i...  57.5 us
    ppermute x7, waiting for transfers between devices, from_behind(): lax.ppermute(value, axis, [(source, source + steps) for source in range(i...  43.4 us
    sub x4, other arithmetic, on_device(): expo = jnp.where(mask, jnp.exp(scores - row_max), 0.0)  23.5 us
    dot_general x4, matrix products, on_device(): jnp.einsum('qgn,nd->qgd', weights, value_part, preferred_element_type=jnp...  12.3 us
    unnamed x24, local copies, waits for them, and re-layouts  6.29 us
    dot_general x4, matrix products, on_device(): jnp.einsum('qgd,nd->qgn', query_part, key_part, preferred_element_type=jn...  4.94 us
  transfers between devices with their start and end apart: 7, of which 3 were waited for; matrix products, arithmetic and copies ran while one was open for 6% of the time, Pallas kernels for 0%

commit v1 on v0

v1 whole, which is shorter than its diff:
```python
import functools
import math

import jax
import jax.numpy as jnp
from jax import lax
from jax.experimental import pallas as pl
from jax.experimental.pallas import tpu as pltpu
from jax.sharding import PartitionSpec as P

H = 16
KVH = 4
HD = 128
GROUP = H // KVH
SPAN = 8
SCALE = math.log2(math.e) / math.sqrt(HD)


def shift(value, steps):
    count = lax.axis_size("ctx")
    return lax.ppermute(value, "ctx", [(s, (s + steps) % count) for s in range(count)])


def doc_starts(doc_ref, positions):
    end = jnp.int32(0)
    starts = jnp.zeros_like(positions)
    for k in range(doc_ref.shape[0]):
        end = end + doc_ref[k]
        starts = jnp.where(end <= positions, end, starts)
    return starts


def attend(first, last, dists, *refs):
    refs = list(refs)
    index_ref, doc_ref, q_ref = refs[:3]
    refs = refs[3:]
    pairs = [(d, refs.pop(0), refs.pop(0)) for d in dists]
    rows = q_ref.shape[0]
    base = index_ref[0] * rows
    if not first:
        m_in, l_in, acc_in = refs[:3]
        refs = refs[3:]
    if last:
        owner_col, owner_row, out_ref, m_ref, l_ref, acc_ref, hot_ref = refs
    else:
        m_ref, l_ref, acc_ref = refs
    positions = base + lax.broadcasted_iota(jnp.int32, (1, rows), 1)
    starts = doc_starts(doc_ref, positions)
    earliest = doc_starts(doc_ref, base)
    key_row = lax.broadcasted_iota(jnp.int32, (rows, rows), 0)

    if not first:
        m_ref[...] = m_in[...]
        l_ref[...] = l_in[...]
        acc_ref[...] = acc_in[...]

    def visit(d, k_ref, v_ref):
        key_pos = base - d * rows + key_row
        visible = key_pos >= starts
        if d == 0:
            visible = visible & (key_pos <= positions)
        k, v = k_ref[...], v_ref[...]
        for g in range(GROUP):
            q = q_ref[:, g * HD : (g + 1) * HD]
            scores = lax.dot_general(
                k, q, (((1,), (1,)), ((), ())), preferred_element_type=jnp.float32
            )
            scores = jnp.where(visible, scores, -jnp.inf)
            top = jnp.max(scores, axis=0, keepdims=True)
            if d > 0:
                before = m_ref[0, g : g + 1, :]
                top = jnp.maximum(before, top)
            expo = jnp.exp2((scores - top) * SCALE)
            total = jnp.sum(expo, axis=0, keepdims=True)
            weighted = lax.dot_general(
                v, expo.astype(jnp.bfloat16), (((0,), (0,)), ((), ())), preferred_element_type=jnp.float32
            )
            if d > 0:
                keep = jnp.exp2((before - top) * SCALE)
                total = l_ref[0, g : g + 1, :] * keep + total
                weighted = acc_ref[0, g * HD : (g + 1) * HD, :] * keep + weighted
            m_ref[0, g : g + 1, :] = top
            l_ref[0, g : g + 1, :] = total
            acc_ref[0, g * HD : (g + 1) * HD, :] = weighted

    for d, k_ref, v_ref in pairs:
        if d == 0:
            visit(d, k_ref, v_ref)
        else:
            pl.when(earliest < base - (d - 1) * rows)(functools.partial(visit, d, k_ref, v_ref))

    if last:
        slots = out_ref.shape[0]

        @pl.when(pl.program_id(0) == 0)
        def _():
            same = (owner_col[...] == owner_row[...]) & (
                key_row < lax.broadcasted_iota(jnp.int32, (rows, rows), 1)
            )
            rank = jnp.sum(same.astype(jnp.int32), axis=0, keepdims=True)
            slot = owner_row[...] * (slots // 32) + rank
            spots = lax.broadcasted_iota(jnp.int32, (slots, rows), 0)
            hot_ref[...] = (spots == slot).astype(jnp.bfloat16)

        for g in range(GROUP):
            attended = acc_ref[0, g * HD : (g + 1) * HD, :] / l_ref[0, g : g + 1, :]
            out_ref[:, g * HD : (g + 1) * HD] = lax.dot_general(
                hot_ref[...], attended.astype(jnp.bfloat16), (((1,), (1,)), ((), ())),
                preferred_element_type=jnp.float32,
            ).astype(jnp.bfloat16)


def step(index, doc_lengths, query_rows, blocks, state=None, owners=None):
    rows, features = query_rows.shape
    first, last = state is None, owners is not None
    dists = [d for d, _, _ in blocks]
    smem = pl.BlockSpec(memory_space=pltpu.SMEM)
    by_head = lambda width: pl.BlockSpec((rows, width), lambda h: (0, h))
    stat = pl.BlockSpec((1, GROUP, rows), lambda h: (h, 0, 0))
    sums = pl.BlockSpec((1, GROUP * HD, rows), lambda h: (h, 0, 0))
    operands, in_specs = [index, doc_lengths, query_rows], [smem, smem, by_head(GROUP * HD)]
    for _, k, v in blocks:
        operands += [k, v]
        in_specs += [by_head(HD), by_head(HD)]
    if not first:
        operands += list(state)
        in_specs += [stat, stat, sums]
    if last:
        slots = 2 * rows
        operands += [owners, owners.reshape(1, rows)]
        in_specs += [pl.BlockSpec((rows, 1), lambda h: (0, 0)), pl.BlockSpec((1, rows), lambda h: (0, 0))]
        out_shape = jax.ShapeDtypeStruct((slots, features), jnp.bfloat16)
        out_specs = pl.BlockSpec((slots, GROUP * HD), lambda h: (0, h))
        scratch = [
            pltpu.VMEM((1, GROUP, rows), jnp.float32),
            pltpu.VMEM((1, GROUP, rows), jnp.float32),
            pltpu.VMEM((1, GROUP * HD, rows), jnp.float32),
            pltpu.VMEM((slots, rows), jnp.bfloat16),
        ]
    else:
        out_shape = [
            jax.ShapeDtypeStruct((KVH, GROUP, rows), jnp.float32),
            jax.ShapeDtypeStruct((KVH, GROUP, rows), jnp.float32),
            jax.ShapeDtypeStruct((KVH, GROUP * HD, rows), jnp.float32),
        ]
        out_specs = [stat, stat, sums]
        scratch = []
    flops = len(dists) * 4 * rows * rows * features
    return pl.pallas_call(
        functools.partial(attend, first, last, dists),
        grid=(KVH,),
        in_specs=in_specs,
        out_specs=out_specs,
        out_shape=out_shape,
        scratch_shapes=scratch,
        compiler_params=pltpu.CompilerParams(vmem_limit_bytes=32 << 20),
        cost_estimate=pl.CostEstimate(
            flops=flops, bytes_accessed=6 << 20, transcendentals=len(dists) * rows * rows * H
        ),
    )(*operands)


def on_device(query_rows, key_rows, value_rows, doc_lengths, row_owner):
    rows, features = query_rows.shape
    devices = lax.axis_size("ctx")
    index = lax.axis_index("ctx").astype(jnp.int32).reshape(1)
    near, far = {0: (key_rows, value_rows)}, {8: (key_rows, value_rows)}
    for hop in range(1, 4):
        near[hop] = tuple(shift(x, 1) for x in near[hop - 1])
        far[8 - hop] = tuple(shift(x, SPAN - 1 if hop == 1 else -1) for x in far[9 - hop])
    middle = (shift(near[3][0], 1), shift(far[5][1], -1))

    state = step(index, doc_lengths, query_rows, [(0, key_rows, value_rows)])
    for hop in range(1, 4):
        state = step(
            index, doc_lengths, query_rows, [(hop, *near[hop]), (8 - hop, *far[8 - hop])], state
        )
    outgoing = step(index, doc_lengths, query_rows, [(4, *middle)], state, row_owner)
    received = lax.all_to_all(
        outgoing.reshape(devices, -1, features), "ctx", split_axis=0, concat_axis=0, tiled=True
    )
    return received.reshape(-1, features)


def solution(mesh):
    rows = P(("dp", "ctx"), None)
    return jax.shard_map(
        on_device,
        mesh=mesh,
        in_specs=(rows, rows, rows, P("dp"), rows),
        out_specs=rows,
        check_vma=False,
    )
```

time: 226 us -> 168 us (0.74)
  the two profiles are of different devices: /device:TPU:456 before, /device:TPU:200 now
where the time goes in v1:
time: 168 us; the launch traced here: 167 us
  blocking collectives  81 us (48%)
  starting transfers between devices  55.2 us (33%)
  Pallas kernels  17.5 us (10%)
  waiting for transfers between devices  6.92 us (4%)
  local copies, waits for them, and re-layouts  5.91 us (4%)
    all_to_all x1, blocking collectives, on_device(): lax.all_to_all(outgoing.reshape(devices, -1, features), 'ctx', split_axis...  81 us
    ppermute x14, starting transfers between devices, shift(): lax.ppermute(value, 'ctx', [(s, (s + steps) % count) for s in range(count)])  55.2 us
    pallas_call x5, Pallas kernels, step(): pl.pallas_call(functools.partial(attend, first, last, dists), grid=(KVH,)...  17.5 us
    ppermute x14, waiting for transfers between devices, shift(): lax.ppermute(value, 'ctx', [(s, (s + steps) % count) for s in range(count)])  6.92 us
    unnamed x12, local copies, waits for them, and re-layouts  5.91 us
  transfers between devices with their start and end apart: 14, of which 2 were waited for; matrix products, arithmetic and copies ran while one was open for 0% of the time, Pallas kernels for 9%

profile of v1, /device:TPU:200, one launch (start us, length us, event | category | flops | bytes accessed | tf_op | source)
XLA Modules:
  0.0 166.9 jit_solution(513213665479850079)
XLA Ops:
  0.0 3.5 %collective-permute-start = (bf16[256,512]{1,0:T(8,128)(2,1)}, bf16[256,512]{1,0:T(8,128)(2,1)S(1)}, u32[]{:S(2)}, u32[]{:S(2)}) collective-permute-start(bf16[256,512]{1,0:T(8,128)(2,1)} %refs_3_.1), channel_id=1, source_target_pairs={{0,1},{1,2},{2,3},{3,4},{4,5},{5,6},{6,7},{7,8},{8,9},{9,10},{10,1... | collective-permute-start | bytes 786440 | tf_op jit(solution)/shard_map/ppermute | solution.py:21
  3.5 3.3 %collective-permute-start.4 = (bf16[256,512]{1,0:T(8,128)(2,1)}, bf16[256,512]{1,0:T(8,128)(2,1)S(1)}, u32[]{:S(2)}, u32[]{:S(2)}) collective-permute-start(bf16[256,512]{1,0:T(8,128)(2,1)} %refs_4_.1), channel_id=1, source_target_pairs={{0,7},{1,8},{2,9},{3,10},{4,11},{5,12},{6,13},{7,14},{8,15},{9,16}... | collective-permute-start | bytes 786440 | tf_op jit(solution)/shard_map/ppermute | solution.py:21
  6.8 3.5 %collective-permute-start.8 = (bf16[256,512]{1,0:T(8,128)(2,1)}, bf16[256,512]{1,0:T(8,128)(2,1)S(1)}, u32[]{:S(2)}, u32[]{:S(2)}) collective-permute-start(bf16[256,512]{1,0:T(8,128)(2,1)} %refs_4_.1), channel_id=1, source_target_pairs={{0,1},{1,2},{2,3},{3,4},{4,5},{5,6},{6,7},{7,8},{8,9},{9,10},{10,1... | collective-permute-start | bytes 786440 | tf_op jit(solution)/shard_map/ppermute | solution.py:21
  10.3 3.3 %collective-permute-start.11 = (bf16[256,512]{1,0:T(8,128)(2,1)}, bf16[256,512]{1,0:T(8,128)(2,1)S(1)}, u32[]{:S(2)}, u32[]{:S(2)}) collective-permute-start(bf16[256,512]{1,0:T(8,128)(2,1)} %refs_3_.1), channel_id=1, source_target_pairs={{0,7},{1,8},{2,9},{3,10},{4,11},{5,12},{6,13},{7,14},{8,15},{9,16}... | collective-permute-start | bytes 786440 | tf_op jit(solution)/shard_map/ppermute | solution.py:21
  13.6 0.0 collective-permute-done.refs_3_
  13.6 3.5 %collective-permute-start.1 = (bf16[256,512]{1,0:T(8,128)(2,1)S(1)}, bf16[256,512]{1,0:T(8,128)(2,1)S(1)}, u32[]{:S(2)}, u32[]{:S(2)}) collective-permute-start(bf16[256,512]{1,0:T(8,128)(2,1)S(1)} %collective-permute-done.refs_3_), channel_id=1, source_target_pairs={{0,1},{1,2},{2,3},{3,4},{4,5},{5,6},{6,7},{7,8},{8,9},{9,10},{10,1... | collective-permute-start | bytes 786440 | tf_op jit(solution)/shard_map/ppermute | solution.py:21
  17.1 5.0 %collective-permute-done.4.refs_6_ = bf16[256,512]{1,0:T(8,128)(2,1)S(1)} collective-permute-done((bf16[256,512]{1,0:T(8,128)(2,1)}, bf16[256,512]{1,0:T(8,128)(2,1)S(1)}, u32[]{:S(2)}, u32[]{:S(2)}) %collective-permute-start.4) | collective-permute-done | bytes 262176 | tf_op jit(solution)/shard_map/ppermute | solution.py:21
  22.0 7.1 %collective-permute-start.5 = (bf16[256,512]{1,0:T(8,128)(2,1)S(1)}, bf16[256,512]{1,0:T(8,128)(2,1)S(1)}, u32[]{:S(2)}, u32[]{:S(2)}) collective-permute-start(bf16[256,512]{1,0:T(8,128)(2,1)S(1)} %collective-permute-done.4.refs_6_), channel_id=1, source_target_pairs={{0,31},{1,0},{2,1},{3,2},{4,3},{5,4},{6,5},{7,6},{8,7},{9,8},{10,9... | collective-permute-start | bytes 786440 | tf_op jit(solution)/shard_map/ppermute | solution.py:21
  29.1 0.0 collective-permute-done.8.refs_4_
  29.1 1.9 %collective-permute-start.9 = (bf16[256,512]{1,0:T(8,128)(2,1)S(1)}, bf16[256,512]{1,0:T(8,128)(2,1)S(1)}, u32[]{:S(2)}, u32[]{:S(2)}) collective-permute-start(bf16[256,512]{1,0:T(8,128)(2,1)S(1)} %collective-permute-done.8.refs_4_), channel_id=1, source_target_pairs={{0,1},{1,2},{2,3},{3,4},{4,5},{5,6},{6,7},{7,8},{8,9},{9,10},{10,1... | collective-permute-start | bytes 786440 | tf_op jit(solution)/shard_map/ppermute | solution.py:21
  31.1 1.9 %collective-permute-done.11.refs_5_ = bf16[256,512]{1,0:T(8,128)(2,1)S(1)} collective-permute-done((bf16[256,512]{1,0:T(8,128)(2,1)}, bf16[256,512]{1,0:T(8,128)(2,1)S(1)}, u32[]{:S(2)}, u32[]{:S(2)}) %collective-permute-start.11) | collective-permute-done | bytes 262176 | tf_op jit(solution)/shard_map/ppermute | solution.py:21
  33.0 7.1 %collective-permute-start.12 = (bf16[256,512]{1,0:T(8,128)(2,1)S(1)}, bf16[256,512]{1,0:T(8,128)(2,1)S(1)}, u32[]{:S(2)}, u32[]{:S(2)}) collective-permute-start(bf16[256,512]{1,0:T(8,128)(2,1)S(1)} %collective-permute-done.11.refs_5_), channel_id=1, source_target_pairs={{0,31},{1,0},{2,1},{3,2},{4,3},{5,4},{6,5},{7,6},{8,7},{9,8},{10,9... | collective-permute-start | bytes 786440 | tf_op jit(solution)/shard_map/ppermute | solution.py:21
  40.1 1.9 %collective-permute-start.2 = (bf16[256,512]{1,0:T(8,128)(2,1)S(1)}, bf16[256,512]{1,0:T(8,128)(2,1)S(1)}, u32[]{:S(2)}, u32[]{:S(2)}) collective-permute-start(bf16[256,512]{1,0:T(8,128)(2,1)S(1)} %collective-permute-done.1.refs_3_), channel_id=1, source_target_pairs={{0,1},{1,2},{2,3},{3,4},{4,5},{5,6},{6,7},{7,8},{8,9},{9,10},{10,1... | collective-permute-start | bytes 786440 | tf_op jit(solution)/shard_map/ppermute | solution.py:21
  42.0 3.9 %collective-permute-start.6 = (bf16[256,512]{1,0:T(8,128)(2,1)S(1)}, bf16[256,512]{1,0:T(8,128)(2,1)S(1)}, u32[]{:S(2)}, u32[]{:S(2)}) collective-permute-start(bf16[256,512]{1,0:T(8,128)(2,1)S(1)} %collective-permute-done.5.refs_6_), channel_id=1, source_target_pairs={{0,31},{1,0},{2,1},{3,2},{4,3},{5,4},{6,5},{7,6},{8,7},{9,8},{10,9... | collective-permute-start | bytes 786440 | tf_op jit(solution)/shard_map/ppermute | solution.py:21
  45.9 1.9 %collective-permute-start.10 = (bf16[256,512]{1,0:T(8,128)(2,1)S(1)}, bf16[256,512]{1,0:T(8,128)(2,1)S(1)}, u32[]{:S(2)}, u32[]{:S(2)}) collective-permute-start(bf16[256,512]{1,0:T(8,128)(2,1)S(1)} %collective-permute-done.9.refs_4_), channel_id=1, source_target_pairs={{0,1},{1,2},{2,3},{3,4},{4,5},{5,6},{6,7},{7,8},{8,9},{9,10},{10,1... | collective-permute-start | bytes 786440 | tf_op jit(solution)/shard_map/ppermute | solution.py:21
  47.9 5.2 %collective-permute-start.13 = (bf16[256,512]{1,0:T(8,128)(2,1)S(1)}, bf16[256,512]{1,0:T(8,128)(2,1)S(1)}, u32[]{:S(2)}, u32[]{:S(2)}) collective-permute-start(bf16[256,512]{1,0:T(8,128)(2,1)S(1)} %collective-permute-done.12.refs_5_), channel_id=1, source_target_pairs={{0,31},{1,0},{2,1},{3,2},{4,3},{5,4},{6,5},{7,6},{8,7},{9,8},{10,9... | collective-permute-start | bytes 786440 | tf_op jit(solution)/shard_map/ppermute | solution.py:21
  53.1 0.8 copy.6.refs_8_
  54.0 0.0 copy-start
  54.0 1.2 copy-done
  55.2 0.7 copy-done.1
  55.8 0.9 copy-done.3
  56.8 0.9 copy-done.4
  57.7 5.9 %shard_map.55 = (f32[4,4,256]{2,1,0:T(4,128)S(1)}, f32[4,4,256]{2,1,0:T(4,128)S(1)}, f32[4,512,256]{2,1,0:T(8,128)S(1)}) custom-call(s32[1]{0:T(128)} %bitcast.refs_0_, s32[18]{0:T(128)S(1)} %copy-done.1, bf16[256,2048]{1,0:T(8,128)(2,1)S(1)} %copy-done, bf16[256,512]{1,0:T(8,128)(2,1)S(1)} %copy-done.3, bf16[256,512]{1,0:T(8,128)(2,1)S(1)} %copy-done.4), custom_call_target="tpu_custom_call" | custom-call | flops 536870912 | bytes 6291456 | tf_op jit(solution)/shard_map/pallas_call | solution.py:149
  63.7 1.9 %collective-permute-start.3 = (bf16[256,512]{1,0:T(8,128)(2,1)S(1)}, bf16[256,512]{1,0:T(8,128)(2,1)S(1)}, u32[]{:S(2)}, u32[]{:S(2)}) collective-permute-start(bf16[256,512]{1,0:T(8,128)(2,1)S(1)} %collective-permute-done.2.refs_3_), channel_id=1, source_target_pairs={{0,1},{1,2},{2,3},{3,4},{4,5},{5,6},{6,7},{7,8},{8,9},{9,10},{10,1... | collective-permute-start | bytes 786440 | tf_op jit(solution)/shard_map/ppermute | solution.py:21
  65.6 7.2 %collective-permute-start.7 = (bf16[256,512]{1,0:T(8,128)(2,1)S(1)}, bf16[256,512]{1,0:T(8,128)(2,1)S(1)}, u32[]{:S(2)}, u32[]{:S(2)}) collective-permute-start(bf16[256,512]{1,0:T(8,128)(2,1)S(1)} %collective-permute-done.6.refs_6_), channel_id=1, source_target_pairs={{0,31},{1,0},{2,1},{3,2},{4,3},{5,4},{6,5},{7,6},{8,7},{9,8},{10,9... | collective-permute-start | bytes 786440 | tf_op jit(solution)/shard_map/ppermute | solution.py:21
  72.9 6.2 %shard_map.56 = (f32[4,4,256]{2,1,0:T(4,128)S(1)}, f32[4,4,256]{2,1,0:T(4,128)S(1)}, f32[4,512,256]{2,1,0:T(8,128)S(1)}) custom-call(s32[1]{0:T(128)} %bitcast.refs_0_, s32[18]{0:T(128)S(1)} %copy-done.1, bf16[256,2048]{1,0:T(8,128)(2,1)S(1)} %copy-done, bf16[256,512]{1,0:T(8,128)(2,1)S(1)} %collective-permute-done.refs_3_, ...), custom_call_target="tpu_custom_call" | custom-call | flops 1073741824 | bytes 6291456 | tf_op jit(solution)/shard_map/pallas_call | solution.py:149
  79.1 1.2 shard_map.57
  80.3 0.0 copy-start.2
  80.3 1.2 shard_map.58
  81.5 3.1 %shard_map.59 = bf16[512,2048]{1,0:T(8,128)(2,1)S(1)} custom-call(s32[1]{0:T(128)} %bitcast.refs_0_, s32[18]{0:T(128)S(1)} %copy-done.1, bf16[256,2048]{1,0:T(8,128)(2,1)S(1)} %copy-done, bf16[256,512]{1,0:T(8,128)(2,1)S(1)} %collective-permute-done.3.refs_3_, bf16[256,512]{1,0:T(8,128)(2,1)S(1)} %collective-permute-done.7.refs_4_, ...), custom_call_target="tpu_custom_call" | custom-call | flops 536870912 | bytes 6291456 | tf_op jit(solution)/shard_map/pallas_call | solution.py:149
  84.6 81.0 %all_to_all.5 = bf16[32,16,2048]{2,1,0:T(8,128)(2,1)S(1)} all-to-all(bf16[32,16,2048]{2,1,0:T(8,128)(2,1)S(1)} %bitcast.4), channel_id=1, replica_groups=mesh['dp'=16,'ctx'=32] {'ctx'}, dimensions={0} | all-to-all | bytes 4194304 | tf_op jit(solution)/shard_map/all_to_all | solution.py:179
  165.6 1.3 copy.8
  (14 shorter events, 0.0 us)
Async XLA Ops:
  0.0 13.6 %collective-permute-start = (bf16[256,512]{1,0:T(8,128)(2,1)}, bf16[256,512]{1,0:T(8,128)(2,1)S(1)}, u32[]{:S(2)}, u32[]{:S(2)}) collective-permute-start(bf16[256,512]{1,0:T(8,128)(2,1)} %refs_3_.1), channel_id=1, source_target_pairs={{0,1},{1,2},{2,3},{3,4},{4,5},{5,6},{6,7},{7,8},{8,9},{9,10},{10,1... | collective-permute-start | bytes 786440 | tf_op jit(solution)/shard_map/ppermute | solution.py:21
  3.5 18.6 %collective-permute-start.4 = (bf16[256,512]{1,0:T(8,128)(2,1)}, bf16[256,512]{1,0:T(8,128)(2,1)S(1)}, u32[]{:S(2)}, u32[]{:S(2)}) collective-permute-start(bf16[256,512]{1,0:T(8,128)(2,1)} %refs_4_.1), channel_id=1, source_target_pairs={{0,7},{1,8},{2,9},{3,10},{4,11},{5,12},{6,13},{7,14},{8,15},{9,16}... | collective-permute-start | bytes 786440 | tf_op jit(solution)/shard_map/ppermute | solution.py:21
  6.8 22.3 %collective-permute-start.8 = (bf16[256,512]{1,0:T(8,128)(2,1)}, bf16[256,512]{1,0:T(8,128)(2,1)S(1)}, u32[]{:S(2)}, u32[]{:S(2)}) collective-permute-start(bf16[256,512]{1,0:T(8,128)(2,1)} %refs_4_.1), channel_id=1, source_target_pairs={{0,1},{1,2},{2,3},{3,4},{4,5},{5,6},{6,7},{7,8},{8,9},{9,10},{10,1... | collective-permute-start | bytes 786440 | tf_op jit(solution)/shard_map/ppermute | solution.py:21
  10.3 22.7 %collective-permute-start.11 = (bf16[256,512]{1,0:T(8,128)(2,1)}, bf16[256,512]{1,0:T(8,128)(2,1)S(1)}, u32[]{:S(2)}, u32[]{:S(2)}) collective-permute-start(bf16[256,512]{1,0:T(8,128)(2,1)} %refs_3_.1), channel_id=1, source_target_pairs={{0,7},{1,8},{2,9},{3,10},{4,11},{5,12},{6,13},{7,14},{8,15},{9,16}... | collective-permute-start | bytes 786440 | tf_op jit(solution)/shard_map/ppermute | solution.py:21
  13.6 26.5 %collective-permute-start.1 = (bf16[256,512]{1,0:T(8,128)(2,1)S(1)}, bf16[256,512]{1,0:T(8,128)(2,1)S(1)}, u32[]{:S(2)}, u32[]{:S(2)}) collective-permute-start(bf16[256,512]{1,0:T(8,128)(2,1)S(1)} %collective-permute-done.refs_3_), channel_id=1, source_target_pairs={{0,1},{1,2},{2,3},{3,4},{4,5},{5,6},{6,7},{7,8},{8,9},{9,10},{10,1... | collective-permute-start | bytes 786440 | tf_op jit(solution)/shard_map/ppermute | solution.py:21
  22.0 19.9 %collective-permute-start.5 = (bf16[256,512]{1,0:T(8,128)(2,1)S(1)}, bf16[256,512]{1,0:T(8,128)(2,1)S(1)}, u32[]{:S(2)}, u32[]{:S(2)}) collective-permute-start(bf16[256,512]{1,0:T(8,128)(2,1)S(1)} %collective-permute-done.4.refs_6_), channel_id=1, source_target_pairs={{0,31},{1,0},{2,1},{3,2},{4,3},{5,4},{6,5},{7,6},{8,7},{9,8},{10,9... | collective-permute-start | bytes 786440 | tf_op jit(solution)/shard_map/ppermute | solution.py:21
  29.1 16.8 %collective-permute-start.9 = (bf16[256,512]{1,0:T(8,128)(2,1)S(1)}, bf16[256,512]{1,0:T(8,128)(2,1)S(1)}, u32[]{:S(2)}, u32[]{:S(2)}) collective-permute-start(bf16[256,512]{1,0:T(8,128)(2,1)S(1)} %collective-permute-done.8.refs_4_), channel_id=1, source_target_pairs={{0,1},{1,2},{2,3},{3,4},{4,5},{5,6},{6,7},{7,8},{8,9},{9,10},{10,1... | collective-permute-start | bytes 786440 | tf_op jit(solution)/shard_map/ppermute | solution.py:21
  33.0 14.9 %collective-permute-start.12 = (bf16[256,512]{1,0:T(8,128)(2,1)S(1)}, bf16[256,512]{1,0:T(8,128)(2,1)S(1)}, u32[]{:S(2)}, u32[]{:S(2)}) collective-permute-start(bf16[256,512]{1,0:T(8,128)(2,1)S(1)} %collective-permute-done.11.refs_5_), channel_id=1, source_target_pairs={{0,31},{1,0},{2,1},{3,2},{4,3},{5,4},{6,5},{7,6},{8,7},{9,8},{10,9... | collective-permute-start | bytes 786440 | tf_op jit(solution)/shard_map/ppermute | solution.py:21
  40.1 23.6 %collective-permute-start.2 = (bf16[256,512]{1,0:T(8,128)(2,1)S(1)}, bf16[256,512]{1,0:T(8,128)(2,1)S(1)}, u32[]{:S(2)}, u32[]{:S(2)}) collective-permute-start(bf16[256,512]{1,0:T(8,128)(2,1)S(1)} %collective-permute-done.1.refs_3_), channel_id=1, source_target_pairs={{0,1},{1,2},{2,3},{3,4},{4,5},{5,6},{6,7},{7,8},{8,9},{9,10},{10,1... | collective-permute-start | bytes 786440 | tf_op jit(solution)/shard_map/ppermute | solution.py:21
  42.0 23.6 %collective-permute-start.6 = (bf16[256,512]{1,0:T(8,128)(2,1)S(1)}, bf16[256,512]{1,0:T(8,128)(2,1)S(1)}, u32[]{:S(2)}, u32[]{:S(2)}) collective-permute-start(bf16[256,512]{1,0:T(8,128)(2,1)S(1)} %collective-permute-done.5.refs_6_), channel_id=1, source_target_pairs={{0,31},{1,0},{2,1},{3,2},{4,3},{5,4},{6,5},{7,6},{8,7},{9,8},{10,9... | collective-permute-start | bytes 786440 | tf_op jit(solution)/shard_map/ppermute | solution.py:21
  45.9 34.3 %collective-permute-start.10 = (bf16[256,512]{1,0:T(8,128)(2,1)S(1)}, bf16[256,512]{1,0:T(8,128)(2,1)S(1)}, u32[]{:S(2)}, u32[]{:S(2)}) collective-permute-start(bf16[256,512]{1,0:T(8,128)(2,1)S(1)} %collective-permute-done.9.refs_4_), channel_id=1, source_target_pairs={{0,1},{1,2},{2,3},{3,4},{4,5},{5,6},{6,7},{7,8},{8,9},{9,10},{10,1... | collective-permute-start | bytes 786440 | tf_op jit(solution)/shard_map/ppermute | solution.py:21
  47.9 32.4 %collective-permute-start.13 = (bf16[256,512]{1,0:T(8,128)(2,1)S(1)}, bf16[256,512]{1,0:T(8,128)(2,1)S(1)}, u32[]{:S(2)}, u32[]{:S(2)}) collective-permute-start(bf16[256,512]{1,0:T(8,128)(2,1)S(1)} %collective-permute-done.12.refs_5_), channel_id=1, source_target_pairs={{0,31},{1,0},{2,1},{3,2},{4,3},{5,4},{6,5},{7,6},{8,7},{9,8},{10,9... | collective-permute-start | bytes 786440 | tf_op jit(solution)/shard_map/ppermute | solution.py:21
  54.0 1.2 copy-start
  55.2 0.7 copy-start.1
  55.8 0.9 copy-start.3
  56.8 0.9 copy-start.4
  63.7 17.8 %collective-permute-start.3 = (bf16[256,512]{1,0:T(8,128)(2,1)S(1)}, bf16[256,512]{1,0:T(8,128)(2,1)S(1)}, u32[]{:S(2)}, u32[]{:S(2)}) collective-permute-start(bf16[256,512]{1,0:T(8,128)(2,1)S(1)} %collective-permute-done.2.refs_3_), channel_id=1, source_target_pairs={{0,1},{1,2},{2,3},{3,4},{4,5},{5,6},{6,7},{7,8},{8,9},{9,10},{10,1... | collective-permute-start | bytes 786440 | tf_op jit(solution)/shard_map/ppermute | solution.py:21
  65.6 15.8 %collective-permute-start.7 = (bf16[256,512]{1,0:T(8,128)(2,1)S(1)}, bf16[256,512]{1,0:T(8,128)(2,1)S(1)}, u32[]{:S(2)}, u32[]{:S(2)}) collective-permute-start(bf16[256,512]{1,0:T(8,128)(2,1)S(1)} %collective-permute-done.6.refs_6_), channel_id=1, source_target_pairs={{0,31},{1,0},{2,1},{3,2},{4,3},{5,4},{6,5},{7,6},{8,7},{9,8},{10,9... | collective-permute-start | bytes 786440 | tf_op jit(solution)/shard_map/ppermute | solution.py:21
  80.3 1.2 copy-start.2

commit v2 on v0

v2 whole, which is shorter than its diff:
```python
import functools
import math

import jax
import jax.numpy as jnp
from jax import lax
from jax.experimental import pallas as pl
from jax.experimental.pallas import tpu as pltpu
from jax.sharding import PartitionSpec as P

H = 16
KVH = 4
HD = 128
GROUP = H // KVH
SPAN = 8
SCALE = math.log2(math.e) / math.sqrt(HD)


def shift(value, steps):
    count = lax.axis_size("ctx")
    return lax.ppermute(value, "ctx", [(s, (s + steps) % count) for s in range(count)])


def doc_start(doc_ref, positions):
    end = jnp.int32(0)
    start = jnp.zeros_like(positions)
    for k in range(doc_ref.shape[0]):
        end = end + doc_ref[k]
        start = jnp.where(end <= positions, end, start)
    return start


def over_group(row):
    return jnp.concatenate([row] * GROUP, axis=1)


def visit(d, base, starts, positions, q_ref, k_ref, v_ref, m_ref, l_ref, acc_ref):
    rows = k_ref.shape[0]
    key_pos = base - d * rows + lax.broadcasted_iota(jnp.int32, (rows, rows), 0)
    visible = key_pos >= starts
    if d == 0:
        visible = visible & (key_pos <= positions)
    scores = lax.dot_general(
        k_ref[...], q_ref[0], (((1,), (0,)), ((), ())), preferred_element_type=jnp.float32
    )
    scores = jnp.where(over_group(visible), scores, -jnp.inf)
    top = jnp.max(scores, axis=0, keepdims=True)
    if d > 0:
        before = m_ref[0]
        top = jnp.maximum(before, top)
    expo = jnp.exp2((scores - top) * SCALE)
    total = jnp.sum(expo, axis=0, keepdims=True)
    weighted = lax.dot_general(
        v_ref[...], expo.astype(jnp.bfloat16), (((0,), (0,)), ((), ())), preferred_element_type=jnp.float32
    )
    if d > 0:
        keep = jnp.exp2((before - top) * SCALE)
        total = l_ref[0] * keep + total
        weighted = acc_ref[0] * keep + weighted
    m_ref[0] = top
    l_ref[0] = total
    acc_ref[0] = weighted


def begin(devices, index_ref, doc_ref, q_ref, k_ref, v_ref, col_ref, row_ref, m_ref, l_ref, acc_ref, hot_ref):
    rows, slots = k_ref.shape[0], hot_ref.shape[0]
    base = index_ref[0] * rows
    positions = base + lax.broadcasted_iota(jnp.int32, (1, rows), 1)
    starts = doc_start(doc_ref, positions)
    visit(0, base, starts, positions, q_ref, k_ref, v_ref, m_ref, l_ref, acc_ref)

    @pl.when(pl.program_id(0) == 0)
    def _():
        earlier = lax.broadcasted_iota(jnp.int32, (rows, rows), 0) < lax.broadcasted_iota(
            jnp.int32, (rows, rows), 1
        )
        same = (col_ref[...] == row_ref[...]) & earlier
        rank = jnp.sum(same.astype(jnp.int32), axis=0, keepdims=True)
        slot = row_ref[...] * (slots // devices) + rank
        spots = lax.broadcasted_iota(jnp.int32, (slots, rows), 0)
        hot_ref[...] = (spots == slot).astype(jnp.float32).astype(jnp.bfloat16)


def proceed(dists, last, index_ref, doc_ref, q_ref, *refs):
    refs = list(refs)
    blocks = [(d, refs.pop(0), refs.pop(0)) for d in dists]
    m_in, l_in, acc_in = refs[:3]
    if last:
        hot_ref, out_ref, m_ref, l_ref, acc_ref = refs[3:]
    else:
        m_ref, l_ref, acc_ref = refs[3:]
    rows = q_ref.shape[2] // GROUP
    base = index_ref[0] * rows
    earliest = doc_start(doc_ref, base)
    m_ref[...] = m_in[...]
    l_ref[...] = l_in[...]
    acc_ref[...] = acc_in[...]

    for d, k_ref, v_ref in blocks:

        @pl.when(earliest < base - (d - 1) * rows)
        def _(d=d, k_ref=k_ref, v_ref=v_ref):
            positions = base + lax.broadcasted_iota(jnp.int32, (1, rows), 1)
            starts = doc_start(doc_ref, positions)
            visit(d, base, starts, positions, q_ref, k_ref, v_ref, m_ref, l_ref, acc_ref)

    if last:
        attended = (acc_ref[0] / l_ref[0]).astype(jnp.bfloat16)
        for g in range(GROUP):
            out_ref[:, g * HD : (g + 1) * HD] = lax.dot_general(
                hot_ref[...], attended[:, g * rows : (g + 1) * rows], (((1,), (1,)), ((), ())),
                preferred_element_type=jnp.float32,
            ).astype(jnp.bfloat16)


SMEM = pl.BlockSpec(memory_space=pltpu.SMEM)


def whole(shape):
    return pl.BlockSpec(shape, lambda h: (0,) * len(shape))


def per_head(*shape):
    return pl.BlockSpec((1, *shape), lambda h: (h, 0, 0))


def block_specs(rows):
    return [pl.BlockSpec((rows, HD), lambda h: (0, h)), pl.BlockSpec((rows, HD), lambda h: (1, h))]


def running(rows):
    sizes = [(1, GROUP * rows), (1, GROUP * rows), (HD, GROUP * rows)]
    return [jax.ShapeDtypeStruct((KVH, *s), jnp.float32) for s in sizes], [per_head(*s) for s in sizes]


def cost(rows, blocks):
    return pl.CostEstimate(
        flops=blocks * 4 * rows * rows * H * HD, bytes_accessed=6 << 20, transcendentals=blocks * rows * rows * H
    )


PARAMS = pltpu.CompilerParams(vmem_limit_bytes=32 << 20)


def first_step(index, doc_lengths, queries, block, row_owner, devices):
    rows = block.shape[0] // 2
    shapes, specs = running(rows)
    return pl.pallas_call(
        functools.partial(begin, devices),
        grid=(KVH,),
        in_specs=[SMEM, SMEM, per_head(HD, GROUP * rows), *block_specs(rows), whole((rows, 1)), whole((1, rows))],
        out_specs=[*specs, whole((2 * rows, rows))],
        out_shape=[*shapes, jax.ShapeDtypeStruct((2 * rows, rows), jnp.bfloat16)],
        compiler_params=PARAMS,
        cost_estimate=cost(rows, 1),
    )(index, doc_lengths, queries, block, block, row_owner, row_owner.reshape(1, rows))


def next_step(index, doc_lengths, queries, blocks, state):
    rows = blocks[0][1].shape[0] // 2
    shapes, specs = running(rows)
    return pl.pallas_call(
        functools.partial(proceed, [d for d, _ in blocks], False),
        grid=(KVH,),
        in_specs=[SMEM, SMEM, per_head(HD, GROUP * rows), *block_specs(rows) * len(blocks), *specs],
        out_specs=specs,
        out_shape=shapes,
        compiler_params=PARAMS,
        cost_estimate=cost(rows, len(blocks)),
    )(index, doc_lengths, queries, *[b for _, block in blocks for b in (block, block)], *state)


def last_step(index, doc_lengths, queries, keys, values, state, hot):
    rows = hot.shape[1]
    _, specs = running(rows)
    flat = pl.BlockSpec((rows, HD), lambda h: (0, h))
    return pl.pallas_call(
        functools.partial(proceed, [SPAN // 2], True),
        grid=(KVH,),
        in_specs=[SMEM, SMEM, per_head(HD, GROUP * rows), flat, flat, *specs, whole(hot.shape)],
        out_specs=pl.BlockSpec((hot.shape[0], GROUP * HD), lambda h: (0, h)),
        out_shape=jax.ShapeDtypeStruct((hot.shape[0], H * HD), jnp.bfloat16),
        scratch_shapes=[pltpu.VMEM(s.block_shape, jnp.float32) for s in specs],
        compiler_params=PARAMS,
        cost_estimate=cost(rows, 1),
    )(index, doc_lengths, queries, keys, values, *state, hot)


def on_device(query_rows, key_rows, value_rows, doc_lengths, row_owner):
    rows, features = query_rows.shape
    devices = lax.axis_size("ctx")
    index = lax.axis_index("ctx").astype(jnp.int32).reshape(1)
    block = jnp.concatenate([key_rows, value_rows], axis=0)
    near, far = shift(block, 1), shift(block, SPAN - 1)
    queries = query_rows.reshape(rows, KVH, GROUP, HD).transpose(1, 3, 2, 0).reshape(KVH, HD, GROUP * rows)
    *state, hot = first_step(index, doc_lengths, queries, block, row_owner, devices)
    for d in range(1, SPAN // 2):
        near, far, *state = lax.optimization_barrier((near, far, *state))
        if d + 1 < SPAN // 2:
            coming = shift(near, 1), shift(far, -1)
        else:
            coming = shift(near[:rows], 1), shift(far[rows:], -1)
        state = next_step(index, doc_lengths, queries, [(d, near), (SPAN - d, far)], state)
        near, far = coming
    outgoing = last_step(index, doc_lengths, queries, near, far, state, hot)
    received = lax.all_to_all(
        outgoing.reshape(devices, -1, features), "ctx", split_axis=0, concat_axis=0, tiled=True
    )
    return received.reshape(-1, features)


def solution(mesh):
    rows = P(("dp", "ctx"), None)
    return jax.shard_map(
        on_device,
        mesh=mesh,
        in_specs=(rows, rows, rows, P("dp"), rows),
        out_specs=rows,
        check_vma=False,
    )
```

time: 226 us -> 143 us (0.63)
  the two profiles are of different devices: /device:TPU:456 before, /device:TPU:200 now
where the time goes in v2:
time: 143 us
  blocking collectives  62.4 us (44%)
  starting transfers between devices  38.4 us (27%)
  waiting for transfers between devices  19.4 us (14%)
  Pallas kernels  12.3 us (9%)
  local copies, waits for them, and re-layouts  9.98 us (7%)
    all_to_all x1, blocking collectives, on_device(): lax.all_to_all(outgoing.reshape(devices, -1, features), 'ctx', split_axis...  62.4 us
    ppermute x8, starting transfers between devices, shift(): lax.ppermute(value, 'ctx', [(s, (s + steps) % count) for s in range(count)])  38.4 us
    ppermute x8, waiting for transfers between devices, shift(): lax.ppermute(value, 'ctx', [(s, (s + steps) % count) for s in range(count)])  19.4 us
    pallas_call x3, Pallas kernels, next_step(): pl.pallas_call(functools.partial(proceed, [d for d, _ in blocks], False),...  6.05 us
    reshape x3, local copies, waits for them, and re-layouts, on_device(): query_rows.reshape(rows, KVH, GROUP, HD).transpose(1, 3, 2, 0)  5.86 us
    pallas_call x1, Pallas kernels, first_step(): pl.pallas_call(functools.partial(begin, devices), grid=(KVH,), in_specs=[...  3.5 us
    unnamed x7, local copies, waits for them, and re-layouts  3.11 us
  transfers between devices with their start and end apart: 8, of which 7 were waited for; matrix products, arithmetic and copies ran while one was open for 5% of the time, Pallas kernels for 7%

profile of v2, /device:TPU:200, one launch (start us, length us, event | category | flops | bytes accessed | tf_op | source)
XLA Modules:
  0.0 142.7 jit_solution(7103271364622561407)
XLA Ops:
  0.0 1.0 constant_dynamic-update-slice_fusion.1
  1.0 1.0 constant_dynamic-update-slice_fusion.k_ref.v_ref
  1.9 3.3 %collective-permute-start.1 = (bf16[512,512]{1,0:T(8,128)(2,1)S(1)}, bf16[512,512]{1,0:T(8,128)(2,1)S(1)}, u32[]{:S(2)}, u32[]{:S(2)}) collective-permute-start(bf16[512,512]{1,0:T(8,128)(2,1)S(1)} %constant_dynamic-update-slice_fusion.k_ref.v_ref), channel_id=1, source_target_pairs={{0,7},{1,8},{2,9},{3,10},{4,11},{5,12},{6,13},{7,14},{8,15},{9,16}... | collective-permute-start | bytes 1572872 | tf_op jit(solution)/shard_map/ppermute | solution.py:21
  5.2 3.5 %collective-permute-start = (bf16[512,512]{1,0:T(8,128)(2,1)S(1)}, bf16[512,512]{1,0:T(8,128)(2,1)S(1)}, u32[]{:S(2)}, u32[]{:S(2)}) collective-permute-start(bf16[512,512]{1,0:T(8,128)(2,1)S(1)} %constant_dynamic-update-slice_fusion.k_ref.v_ref), channel_id=1, source_target_pairs={{0,1},{1,2},{2,3},{3,4},{4,5},{5,6},{6,7},{7,8},{8,9},{9,10},{10,1... | collective-permute-start | bytes 1572872 | tf_op jit(solution)/shard_map/ppermute | solution.py:21
  8.7 0.8 copy.7.col_ref
  9.5 1.8 %reshape.19 = bf16[256,4,4,128]{3,2,1,0:T(4,128)(2,1)S(1)} reshape(bf16[256,2048]{1,0:T(8,128)(2,1)} %param.5) | data formatting | bytes 2097152 | tf_op jit(solution)/shard_map/reshape | solution.py:195
  11.3 0.0 copy-start
  11.4 0.0 copy-start.1
  11.4 2.3 %copy.6 = bf16[256,4,4,128]{0,2,3,1:T(4,128)(2,1)} copy(bf16[256,4,4,128]{3,2,1,0:T(4,128)(2,1)S(1)} %reshape.19) | data formatting | bytes 2097152 | tf_op jit(solution)/shard_map/reshape | solution.py:195
  13.7 1.8 %reshape.20.q_ref = bf16[4,128,1024]{2,1,0:T(8,128)(2,1)S(1)} reshape(bf16[4,128,4,256]{3,2,1,0:T(4,128)(2,1)} %bitcast.8) | data formatting | bytes 2097152 | tf_op jit(solution)/shard_map/reshape | solution.py:195
  15.5 0.0 copy-done
  15.5 3.5 %shard_map.55 = (f32[4,1,1024]{2,1,0:T(1,128)S(1)}, f32[4,1,1024]{2,1,0:T(1,128)S(1)}, f32[4,128,1024]{2,1,0:T(8,128)S(1)}, bf16[512,256]{1,0:T(8,128)(2,1)S(1)}) custom-call(s32[1]{0:T(128)} %bitcast.index_ref, s32[18]{0:T(128)S(1)} %copy-done, bf16[4,128,1024]{2,1,0:T(8,128)(2,1)S(1)} %reshape.20.q_ref, ...), custom_call_target="tpu_custom_call" | custom-call | flops 536870912 | bytes 6291456 | tf_op jit(solution)/shard_map/pallas_call | solution.py:148
  19.0 3.0 %collective-permute-done.1.refs_2_.refs_3_ = bf16[512,512]{1,0:T(8,128)(2,1)S(1)} collective-permute-done((bf16[512,512]{1,0:T(8,128)(2,1)S(1)}, bf16[512,512]{1,0:T(8,128)(2,1)S(1)}, u32[]{:S(2)}, u32[]{:S(2)}) %collective-permute-start.1) | collective-permute-done | bytes 524320 | tf_op jit(solution)/shard_map/ppermute | solution.py:21
  22.0 0.0 collective-permute-done.refs_0_.refs_1_
  22.0 2.0 %collective-permute-start.2 = (bf16[512,512]{1,0:T(8,128)(2,1)S(1)}, bf16[512,512]{1,0:T(8,128)(2,1)S(1)}, u32[]{:S(2)}, u32[]{:S(2)}) collective-permute-start(bf16[512,512]{1,0:T(8,128)(2,1)S(1)} %collective-permute-done.refs_0_.refs_1_), channel_id=1, source_target_pairs={{0,1},{1,2},{2,3},{3,4},{4,5},{5,6},{6,7},{7,8},{8,9},{9,10},{10,1... | collective-permute-start | bytes 1572872 | tf_op jit(solution)/shard_map/ppermute | solution.py:21
  24.0 11.1 %collective-permute-start.3 = (bf16[512,512]{1,0:T(8,128)(2,1)S(1)}, bf16[512,512]{1,0:T(8,128)(2,1)S(1)}, u32[]{:S(2)}, u32[]{:S(2)}) collective-permute-start(bf16[512,512]{1,0:T(8,128)(2,1)S(1)} %collective-permute-done.1.refs_2_.refs_3_), channel_id=1, source_target_pairs={{0,31},{1,0},{2,1},{3,2},{4,3},{5,4},{6,5},{7,6},{8,7},{9,8},{10,9... | collective-permute-start | bytes 1572872 | tf_op jit(solution)/shard_map/ppermute | solution.py:21
  35.1 3.9 %shard_map.56 = (f32[4,1,1024]{2,1,0:T(1,128)S(1)}, f32[4,1,1024]{2,1,0:T(1,128)S(1)}, f32[4,128,1024]{2,1,0:T(8,128)S(1)}) custom-call(s32[1]{0:T(128)} %bitcast.index_ref, s32[18]{0:T(128)S(1)} %copy-done, bf16[4,128,1024]{2,1,0:T(8,128)(2,1)S(1)} %reshape.20.q_ref, bf16[512,512]{1,0:T(8,128)(2,1)S(1)} %collective-permute-done.refs_0_.refs_1_, ...), custom_call_target="tpu_custom_call" | custom-call | flops 1073741824 | bytes 6291456 | tf_op jit(solution)/shard_map/pallas_call | solution.py:162
  39.1 4.8 %collective-permute-done.2.refs_0_.refs_1_ = bf16[512,512]{1,0:T(8,128)(2,1)S(1)} collective-permute-done((bf16[512,512]{1,0:T(8,128)(2,1)S(1)}, bf16[512,512]{1,0:T(8,128)(2,1)S(1)}, u32[]{:S(2)}, u32[]{:S(2)}) %collective-permute-start.2) | collective-permute-done | bytes 524320 | tf_op jit(solution)/shard_map/ppermute | solution.py:21
  43.9 1.2 collective-permute-done.3.refs_2_.refs_3_
  45.0 1.9 %collective-permute-start.4 = (bf16[512,512]{1,0:T(8,128)(2,1)S(1)}, bf16[512,512]{1,0:T(8,128)(2,1)S(1)}, u32[]{:S(2)}, u32[]{:S(2)}) collective-permute-start(bf16[512,512]{1,0:T(8,128)(2,1)S(1)} %collective-permute-done.2.refs_0_.refs_1_), channel_id=1, source_target_pairs={{0,1},{1,2},{2,3},{3,4},{4,5},{5,6},{6,7},{7,8},{8,9},{9,10},{10,1... | collective-permute-start | bytes 1572872 | tf_op jit(solution)/shard_map/ppermute | solution.py:21
  47.0 7.0 %collective-permute-start.5 = (bf16[512,512]{1,0:T(8,128)(2,1)S(1)}, bf16[512,512]{1,0:T(8,128)(2,1)S(1)}, u32[]{:S(2)}, u32[]{:S(2)}) collective-permute-start(bf16[512,512]{1,0:T(8,128)(2,1)S(1)} %collective-permute-done.3.refs_2_.refs_3_), channel_id=1, source_target_pairs={{0,31},{1,0},{2,1},{3,2},{4,3},{5,4},{6,5},{7,6},{8,7},{9,8},{10,9... | collective-permute-start | bytes 1572872 | tf_op jit(solution)/shard_map/ppermute | solution.py:21
  53.9 1.1 shard_map.57
  55.0 6.5 %collective-permute-done.4.refs_0_.refs_1_ = bf16[512,512]{1,0:T(8,128)(2,1)S(1)} collective-permute-done((bf16[512,512]{1,0:T(8,128)(2,1)S(1)}, bf16[512,512]{1,0:T(8,128)(2,1)S(1)}, u32[]{:S(2)}, u32[]{:S(2)}) %collective-permute-start.4) | collective-permute-done | bytes 524320 | tf_op jit(solution)/shard_map/ppermute | solution.py:21
  61.5 1.2 collective-permute-done.5.refs_2_.refs_3_
  62.7 1.9 %collective-permute-start.6 = (bf16[256,512]{1,0:T(8,128)(2,1)S(1)}, bf16[256,512]{1,0:T(8,128)(2,1)S(1)}, u32[]{:S(2)}, u32[]{:S(2)}) collective-permute-start(bf16[256,512]{1,0:T(8,128)(2,1)S(1)} %slice.6), channel_id=1, source_target_pairs={{0,1},{1,2},{2,3},{3,4},{4,5},{5,6},{6,7},{7,8},{8,9},{9,10},{10,1... | collective-permute-start | bytes 786440 | tf_op jit(solution)/shard_map/ppermute | solution.py:21
  64.6 7.7 %collective-permute-start.7 = (bf16[256,512]{1,0:T(8,128)(2,1)S(1)}, bf16[256,512]{1,0:T(8,128)(2,1)S(1)}, u32[]{:S(2)}, u32[]{:S(2)}) collective-permute-start(bf16[256,512]{1,0:T(8,128)(2,1)S(1)} %slice.7), channel_id=1, source_target_pairs={{0,31},{1,0},{2,1},{3,2},{4,3},{5,4},{6,5},{7,6},{8,7},{9,8},{10,9... | collective-permute-start | bytes 786440 | tf_op jit(solution)/shard_map/ppermute | solution.py:21
  72.3 1.1 shard_map.58
  73.4 1.3 collective-permute-done.6.refs_0_
  74.7 1.5 %collective-permute-done.7.refs_1_ = bf16[256,512]{1,0:T(8,128)(2,1)S(1)} collective-permute-done((bf16[256,512]{1,0:T(8,128)(2,1)S(1)}, bf16[256,512]{1,0:T(8,128)(2,1)S(1)}, u32[]{:S(2)}, u32[]{:S(2)}) %collective-permute-start.7) | collective-permute-done | bytes 262176 | tf_op jit(solution)/shard_map/ppermute | solution.py:21
  76.2 2.7 %shard_map.59 = bf16[512,2048]{1,0:T(8,128)(2,1)S(1)} custom-call(s32[1]{0:T(128)} %bitcast.index_ref, s32[18]{0:T(128)S(1)} %copy-done, bf16[4,128,1024]{2,1,0:T(8,128)(2,1)S(1)} %reshape.20.q_ref, bf16[256,512]{1,0:T(8,128)(2,1)S(1)} %collective-permute-done.6.refs_0_, bf16[256,512]{1,0:T(8,128)(2,1)S(1)} %collective-permute-done.7.refs_1_, ...), custom_call_target="tpu_custom_call" | custom-call | flops 536870912 | bytes 6291456 | tf_op jit(solution)/shard_map/pallas_call | solution.py:177
  78.9 62.4 %all_to_all.5 = bf16[32,16,2048]{2,1,0:T(8,128)(2,1)S(1)} all-to-all(bf16[32,16,2048]{2,1,0:T(8,128)(2,1)S(1)} %bitcast.5), channel_id=1, replica_groups=mesh['dp'=16,'ctx'=32] {'ctx'}, dimensions={0} | all-to-all | bytes 4194304 | tf_op jit(solution)/shard_map/all_to_all | solution.py:206
  141.4 1.3 copy.10
  (3 shorter events, 0.0 us)
Async XLA Ops:
  1.9 20.0 %collective-permute-start.1 = (bf16[512,512]{1,0:T(8,128)(2,1)S(1)}, bf16[512,512]{1,0:T(8,128)(2,1)S(1)}, u32[]{:S(2)}, u32[]{:S(2)}) collective-permute-start(bf16[512,512]{1,0:T(8,128)(2,1)S(1)} %constant_dynamic-update-slice_fusion.k_ref.v_ref), channel_id=1, source_target_pairs={{0,7},{1,8},{2,9},{3,10},{4,11},{5,12},{6,13},{7,14},{8,15},{9,16}... | collective-permute-start | bytes 1572872 | tf_op jit(solution)/shard_map/ppermute | solution.py:21
  5.2 16.7 %collective-permute-start = (bf16[512,512]{1,0:T(8,128)(2,1)S(1)}, bf16[512,512]{1,0:T(8,128)(2,1)S(1)}, u32[]{:S(2)}, u32[]{:S(2)}) collective-permute-start(bf16[512,512]{1,0:T(8,128)(2,1)S(1)} %constant_dynamic-update-slice_fusion.k_ref.v_ref), channel_id=1, source_target_pairs={{0,1},{1,2},{2,3},{3,4},{4,5},{5,6},{6,7},{7,8},{8,9},{9,10},{10,1... | collective-permute-start | bytes 1572872 | tf_op jit(solution)/shard_map/ppermute | solution.py:21
  11.3 4.1 %copy-start = (s32[18]{0:T(128)S(1)}, s32[18]{0:T(128)}, u32[]{:S(2)}) copy-start(s32[18]{0:T(128)} %doc_ref.9) | copy-start | bytes 220
  11.4 4.1 %copy-start.1 = (s32[256,1]{0,1:T(1,128)S(1)}, s32[256,1]{0,1:T(1,128)}, u32[]{:S(2)}) copy-start(s32[256,1]{0,1:T(1,128)} %param.9) | copy-start | bytes 3076
  22.0 21.9 %collective-permute-start.2 = (bf16[512,512]{1,0:T(8,128)(2,1)S(1)}, bf16[512,512]{1,0:T(8,128)(2,1)S(1)}, u32[]{:S(2)}, u32[]{:S(2)}) collective-permute-start(bf16[512,512]{1,0:T(8,128)(2,1)S(1)} %collective-permute-done.refs_0_.refs_1_), channel_id=1, source_target_pairs={{0,1},{1,2},{2,3},{3,4},{4,5},{5,6},{6,7},{7,8},{8,9},{9,10},{10,1... | collective-permute-start | bytes 1572872 | tf_op jit(solution)/shard_map/ppermute | solution.py:21
  24.0 21.0 %collective-permute-start.3 = (bf16[512,512]{1,0:T(8,128)(2,1)S(1)}, bf16[512,512]{1,0:T(8,128)(2,1)S(1)}, u32[]{:S(2)}, u32[]{:S(2)}) collective-permute-start(bf16[512,512]{1,0:T(8,128)(2,1)S(1)} %collective-permute-done.1.refs_2_.refs_3_), channel_id=1, source_target_pairs={{0,31},{1,0},{2,1},{3,2},{4,3},{5,4},{6,5},{7,6},{8,7},{9,8},{10,9... | collective-permute-start | bytes 1572872 | tf_op jit(solution)/shard_map/ppermute | solution.py:21
  45.0 16.4 %collective-permute-start.4 = (bf16[512,512]{1,0:T(8,128)(2,1)S(1)}, bf16[512,512]{1,0:T(8,128)(2,1)S(1)}, u32[]{:S(2)}, u32[]{:S(2)}) collective-permute-start(bf16[512,512]{1,0:T(8,128)(2,1)S(1)} %collective-permute-done.2.refs_0_.refs_1_), channel_id=1, source_target_pairs={{0,1},{1,2},{2,3},{3,4},{4,5},{5,6},{6,7},{7,8},{8,9},{9,10},{10,1... | collective-permute-start | bytes 1572872 | tf_op jit(solution)/shard_map/ppermute | solution.py:21
  47.0 15.7 %collective-permute-start.5 = (bf16[512,512]{1,0:T(8,128)(2,1)S(1)}, bf16[512,512]{1,0:T(8,128)(2,1)S(1)}, u32[]{:S(2)}, u32[]{:S(2)}) collective-permute-start(bf16[512,512]{1,0:T(8,128)(2,1)S(1)} %collective-permute-done.3.refs_2_.refs_3_), channel_id=1, source_target_pairs={{0,31},{1,0},{2,1},{3,2},{4,3},{5,4},{6,5},{7,6},{8,7},{9,8},{10,9... | collective-permute-start | bytes 1572872 | tf_op jit(solution)/shard_map/ppermute | solution.py:21
  62.7 12.1 %collective-permute-start.6 = (bf16[256,512]{1,0:T(8,128)(2,1)S(1)}, bf16[256,512]{1,0:T(8,128)(2,1)S(1)}, u32[]{:S(2)}, u32[]{:S(2)}) collective-permute-start(bf16[256,512]{1,0:T(8,128)(2,1)S(1)} %slice.6), channel_id=1, source_target_pairs={{0,1},{1,2},{2,3},{3,4},{4,5},{5,6},{6,7},{7,8},{8,9},{9,10},{10,1... | collective-permute-start | bytes 786440 | tf_op jit(solution)/shard_map/ppermute | solution.py:21
  64.6 11.6 %collective-permute-start.7 = (bf16[256,512]{1,0:T(8,128)(2,1)S(1)}, bf16[256,512]{1,0:T(8,128)(2,1)S(1)}, u32[]{:S(2)}, u32[]{:S(2)}) collective-permute-start(bf16[256,512]{1,0:T(8,128)(2,1)S(1)} %slice.7), channel_id=1, source_target_pairs={{0,31},{1,0},{2,1},{3,2},{4,3},{5,4},{6,5},{7,6},{8,7},{9,8},{10,9... | collective-permute-start | bytes 786440 | tf_op jit(solution)/shard_map/ppermute | solution.py:21

commit v3 on v0

v3 whole, which is shorter than its diff:
```python
import functools
import math

import jax
import jax.numpy as jnp
from jax import lax
from jax.experimental import pallas as pl
from jax.experimental.pallas import tpu as pltpu
from jax.sharding import PartitionSpec as P

H = 16
KVH = 4
HD = 128
GROUP = H // KVH
TEAM = 4
PAD = 16
SCALE = math.log2(math.e) / math.sqrt(HD)
NT = (((1,), (1,)), ((), ()))
SMEM = pl.BlockSpec(memory_space=pltpu.SMEM)
VMEM = pl.BlockSpec(memory_space=pltpu.VMEM)


def doc_start(doc_ref, positions):
    end = jnp.int32(0)
    start = jnp.zeros_like(positions)
    for k in range(doc_ref.shape[0]):
        end = end + doc_ref[k]
        start = jnp.where(end <= positions, end, start)
    return start


def split(index_ref, q_ref, k_ref, v_ref, owner_ref, kv_out, q_out):
    rows = k_ref.shape[0]
    odd = lax.rem(lax.div(index_ref[0], TEAM), 2) == 1
    owners = jnp.broadcast_to(owner_ref[...], (PAD, rows)).astype(jnp.float32).astype(jnp.bfloat16)
    for h in range(KVH):
        member = jnp.where(odd, KVH - 1 - h, h)
        head = slice(h * HD, (h + 1) * HD)
        kv_out[member, :rows, :HD] = k_ref[:, head]
        kv_out[member, :rows, HD:] = v_ref[:, head]
        kv_out[member, rows:, :] = owners
        q_out[member] = q_ref[:, h * GROUP * HD : (h + 1) * GROUP * HD]


def over_group(row):
    return jnp.concatenate([row] * GROUP, axis=1)


def attend(devices, index_ref, doc_ref, q_ref, own_ref, back_ref, far_ref, out_ref, q_t, m_ref, l_ref, acc_ref):
    i = pl.program_id(0)
    rows = q_ref.shape[1]
    first_shard = lax.div(index_ref[0], TEAM) * TEAM
    base = (first_shard + i) * rows
    positions = base + lax.broadcasted_iota(jnp.int32, (1, rows), 1)
    starts = doc_start(doc_ref, positions)
    turned = q_ref[0].T
    q_t[...] = jnp.concatenate([turned[g * HD : (g + 1) * HD] for g in range(GROUP)], axis=1)

    def visit(block_ref, place, shard, first):
        k, v = block_ref[place, :rows, :HD], block_ref[place, :rows, HD:]
        key_pos = (first_shard + shard) * rows + lax.broadcasted_iota(jnp.int32, (rows, rows), 0)
        visible = key_pos >= starts
        if first:
            visible = visible & (key_pos <= positions)
        scores = jnp.dot(k, q_t[...], preferred_element_type=jnp.float32)
        scores = jnp.where(over_group(visible), scores, -jnp.inf)
        top = jnp.max(scores, axis=0, keepdims=True)
        if not first:
            before = m_ref[...]
            top = jnp.maximum(before, top)
        expo = jnp.exp2((scores - top) * SCALE)
        total = jnp.sum(expo, axis=0, keepdims=True)
        weighted = lax.dot_general(
            v, expo.astype(jnp.bfloat16), (((0,), (0,)), ((), ())), preferred_element_type=jnp.float32
        )
        if not first:
            keep = jnp.exp2((before - top) * SCALE)
            total = l_ref[...] * keep + total
            weighted = acc_ref[...] * keep + weighted
        m_ref[...] = top
        l_ref[...] = total
        acc_ref[...] = weighted

    visit(own_ref, i, i, True)
    lowest = jnp.maximum(lax.div(doc_start(doc_ref, base), rows) - first_shard, i - 7)
    for ref, low in ((own_ref, 0), (back_ref, -TEAM), (far_ref, -2 * TEAM)):

        @pl.loop(jnp.maximum(lowest, low), jnp.minimum(i, low + TEAM))
        def _(shard, ref=ref, low=low):
            visit(ref, shard - low, shard, False)

    owner_row = own_ref[i, rows : rows + PAD, :][:1].astype(jnp.float32)
    across = jnp.broadcast_to(owner_row, (rows, rows))
    earlier = lax.broadcasted_iota(jnp.int32, (rows, rows), 0) < lax.broadcasted_iota(jnp.int32, (rows, rows), 1)
    same = (across == across.T) & earlier
    rank = jnp.sum(same.astype(jnp.int32), axis=0, keepdims=True)
    slots = 2 * rows
    slot = owner_row.astype(jnp.int32) * (slots // devices) + rank
    spots = lax.broadcasted_iota(jnp.int32, (slots, rows), 0)
    hot = (spots == slot).astype(jnp.float32).astype(jnp.bfloat16)
    attended = (acc_ref[...] / l_ref[...]).astype(jnp.bfloat16)
    attended = jnp.concatenate([attended[:, g * rows : (g + 1) * rows] for g in range(GROUP)], axis=0)
    placed = lax.dot_general(hot, attended, NT, preferred_element_type=jnp.float32).astype(jnp.bfloat16)
    out_ref[:, 0] = placed.reshape(devices, slots // devices, GROUP * HD)


def gather_heads(in_ref, out_ref):
    depth, width = in_ref.shape[1:]
    for team in range(2):
        for member in range(TEAM):
            h = KVH - 1 - member if team else member
            out_ref[team * depth : (team + 1) * depth, h * width : (h + 1) * width] = in_ref[team * TEAM + member]


def on_device(query_rows, key_rows, value_rows, doc_lengths, row_owner):
    rows, features = query_rows.shape
    devices = lax.axis_size("ctx")
    teams = devices // TEAM
    index = lax.axis_index("ctx").astype(jnp.int32).reshape(1)
    params = pltpu.CompilerParams(vmem_limit_bytes=40 << 20)
    groups = [[t * TEAM + m for m in range(TEAM)] for t in range(teams)]
    width = GROUP * HD

    kv, queries = pl.pallas_call(
        split,
        in_specs=[SMEM] + [VMEM] * 4,
        out_specs=[VMEM] * 2,
        out_shape=[
            jax.ShapeDtypeStruct((TEAM, rows + PAD, 2 * HD), jnp.bfloat16),
            jax.ShapeDtypeStruct((TEAM, rows, width), jnp.bfloat16),
        ],
        compiler_params=params,
    )(index, query_rows, key_rows, value_rows, row_owner.reshape(1, rows))
    own = lax.all_to_all(kv, "ctx", 0, 0, axis_index_groups=groups, tiled=True)
    own, queries = lax.optimization_barrier((own, queries))
    back = lax.ppermute(
        own, "ctx",
        [(t * TEAM + m, (t + 1) * TEAM + TEAM - 1 - m) for t in range(teams - 1) for m in range(TEAM)],
    )
    far = lax.ppermute(own, "ctx", [(s, s + 2 * TEAM) for s in range(devices - 2 * TEAM)])
    queries = lax.all_to_all(queries, "ctx", 0, 0, axis_index_groups=groups, tiled=True)

    slots = 2 * rows // devices
    outgoing = pl.pallas_call(
        functools.partial(attend, devices),
        grid=(TEAM,),
        in_specs=[SMEM, SMEM, pl.BlockSpec((1, rows, width), lambda i: (i, 0, 0)), VMEM, VMEM, VMEM],
        out_specs=pl.BlockSpec((devices, 1, slots, width), lambda i: (0, i, 0, 0)),
        out_shape=jax.ShapeDtypeStruct((devices, TEAM, slots, width), jnp.bfloat16),
        scratch_shapes=[
            pltpu.VMEM((HD, GROUP * rows), jnp.bfloat16),
            pltpu.VMEM((1, GROUP * rows), jnp.float32),
            pltpu.VMEM((1, GROUP * rows), jnp.float32),
            pltpu.VMEM((HD, GROUP * rows), jnp.float32),
        ],
        compiler_params=params,
    )(index, doc_lengths, queries, own, back, far)
    received = lax.all_to_all(
        outgoing.reshape(devices, TEAM * slots, width), "ctx", split_axis=0, concat_axis=0, tiled=True
    )
    return pl.pallas_call(
        gather_heads,
        grid=(teams // 2,),
        in_specs=[pl.BlockSpec((2 * TEAM, TEAM * slots, width), lambda t: (t, 0, 0))],
        out_specs=pl.BlockSpec((2 * TEAM * slots, features), lambda t: (t, 0)),
        out_shape=jax.ShapeDtypeStruct((devices * slots, features), jnp.bfloat16),
        compiler_params=params,
    )(received)


def solution(mesh):
    rows = P(("dp", "ctx"), None)
    return jax.shard_map(
        on_device,
        mesh=mesh,
        in_specs=(rows, rows, rows, P("dp"), rows),
        out_specs=rows,
        check_vma=False,
    )
```

time: 226 us -> 139 us (0.62)
  starting transfers between devices: 57.5 us -> 14.2 us
  other arithmetic: 33.3 us -> 0 us
  blocking collectives: 62.8 us -> 90.7 us
  waiting for transfers between devices: 43.4 us -> 19 us
  matrix products: 17.3 us -> 0 us
  Pallas kernels: 0 us -> 11 us
  local copies, waits for them, and re-layouts: 10.6 us -> 3.81 us
    ppermute x7 -> x2, starting transfers between devices: 57.5 us -> 9.17 us  [the longest x1 5.75 us: on_device(): lax.ppermute(own, 'ctx', [(t * TEAM + m, (t + 1) * TEAM + TEAM - 1 - m) f...]
    all_to_all x1 -> x2, blocking collectives: 62.8 us -> 90.7 us  [the longest x1 71.9 us: on_device(): lax.all_to_all(outgoing.reshape(devices, TEAM * slots, width), 'ctx', spl...]
    ppermute x7 -> x2, waiting for transfers between devices: 43.4 us -> 19 us  [the longest x1 13.3 us: on_device(): lax.ppermute(own, 'ctx', [(t * TEAM + m, (t + 1) * TEAM + TEAM - 1 - m) f...]
    sub x4 -> x0, other arithmetic: 23.5 us -> none  [on_device(): expo = jnp.where(mask, jnp.exp(scores - row_max), 0.0)]
    dot_general x8 -> x0, matrix products: 17.3 us -> none  [the longest x4 12.3 us: on_device(): jnp.einsum('qgn,nd->qgd', weights, value_part, preferred_element_type=jnp...]
    pallas_call x0 -> x3, Pallas kernels: none -> 11 us  [the longest x1 8.07 us: on_device(): pl.pallas_call(functools.partial(attend, devices), grid=(TEAM,), in_specs...]
    all_to_all x0 -> x1, starting transfers between devices: none -> 5.03 us  [on_device(): lax.all_to_all(queries, 'ctx', 0, 0, axis_index_groups=groups, tiled=True)]
    scatter x1 -> x0, other arithmetic: 2.91 us -> none  [on_device(): jnp.zeros((devices * pair_slots, features), jnp.bfloat16).at[send_slot]]
  transfers between devices with their start and end apart: 7 -> 3, of which waited for: 3 -> 2; matrix products, arithmetic and copies ran while one was open for 6% -> 0% of each run, Pallas kernels for 0% -> 0%
where the time goes in v3:
time: 139 us
  blocking collectives  90.7 us (65%)
  waiting for transfers between devices  19 us (14%)
  starting transfers between devices  14.2 us (10%)
  Pallas kernels  11 us (8%)
  local copies, waits for them, and re-layouts  3.81 us (3%)
    all_to_all x1, blocking collectives, on_device(): lax.all_to_all(outgoing.reshape(devices, TEAM * slots, width), 'ctx', spl...  71.9 us
    all_to_all x1, blocking collectives, on_device(): own = lax.all_to_all(kv, 'ctx', 0, 0, axis_index_groups=groups, tiled=True)  18.8 us
    ppermute x1, waiting for transfers between devices, on_device(): lax.ppermute(own, 'ctx', [(t * TEAM + m, (t + 1) * TEAM + TEAM - 1 - m) f...  13.3 us
    pallas_call x1, Pallas kernels, on_device(): pl.pallas_call(functools.partial(attend, devices), grid=(TEAM,), in_specs...  8.07 us
    ppermute x1, starting transfers between devices, on_device(): lax.ppermute(own, 'ctx', [(t * TEAM + m, (t + 1) * TEAM + TEAM - 1 - m) f...  5.75 us
    ppermute x1, waiting for transfers between devices, on_device(): lax.ppermute(own, 'ctx', [(s, s + 2 * TEAM) for s in range(devices - 2 *...  5.68 us
    all_to_all x1, starting transfers between devices, on_device(): lax.all_to_all(queries, 'ctx', 0, 0, axis_index_groups=groups, tiled=True)  5.03 us
    unnamed x10, local copies, waits for them, and re-layouts  3.81 us
  transfers between devices with their start and end apart: 3, of which 2 were waited for; matrix products, arithmetic and copies ran while one was open for 0% of the time, Pallas kernels for 0%

profile of v3, /device:TPU:456, one launch (start us, length us, event | category | flops | bytes accessed | tf_op | source)
XLA Modules:
  0.0 138.7 jit_solution(11549225705202703049)
XLA Ops:
  0.0 0.0 copy-start
  0.0 1.2 copy-done
  1.2 0.0 copy-start.1
  1.2 0.9 copy-done.1
  2.2 0.0 copy-start.2
  2.2 0.9 copy-done.2
  3.1 0.0 copy-start.3
  3.1 0.7 copy-done.3
  3.8 0.0 copy-start.4
  3.8 1.1 shard_map.55
  4.9 18.8 %all_to_all.15.own_ref = bf16[4,272,256]{2,1,0:T(8,128)(2,1)S(1)} all-to-all(bf16[4,272,256]{2,1,0:T(8,128)(2,1)S(1)} %get-tuple-element.9), channel_id=1, replica_groups={{0,1,2,3},{4,5,6,7},{8,9,10,11},{12,13,14,15},{16,17,18,19},{20,21,22,2..., dimensions={0} | all-to-all | bytes 1114112 | tf_op jit(solution)/shard_map/all_to_all | solution.py:134
  23.7 5.0 %all-to-all-start.1 = ((bf16[4,256,512]{2,1,0:T(8,128)(2,1)}), bf16[4,256,512]{2,1,0:T(8,128)(2,1)S(1)}, u32[]{:S(2)}, u32[]{:S(2)}) async-start(bf16[4,256,512]{2,1,0:T(8,128)(2,1)} %get-tuple-element.11), calls=%async_computation.1 | async-start | bytes 2097152 | tf_op jit(solution)/shard_map/all_to_all | solution.py:141
  28.7 3.4 %collective-permute-start.1 = (bf16[4,272,256]{2,1,0:T(8,128)(2,1)S(1)}, bf16[4,272,256]{2,1,0:T(8,128)(2,1)S(1)}, u32[]{:S(2)}, u32[]{:S(2)}) collective-permute-start(bf16[4,272,256]{2,1,0:T(8,128)(2,1)S(1)} %all_to_all.15.own_ref), channel_id=1, source_target_pairs={{0,8},{1,9},{2,10},{3,11},{4,12},{5,13},{6,14},{7,15},{8,16},{9,17... | collective-permute-start | bytes 1671176 | tf_op jit(solution)/shard_map/ppermute | solution.py:140
  32.2 5.7 %collective-permute-start = (bf16[4,272,256]{2,1,0:T(8,128)(2,1)S(1)}, bf16[4,272,256]{2,1,0:T(8,128)(2,1)S(1)}, u32[]{:S(2)}, u32[]{:S(2)}) collective-permute-start(bf16[4,272,256]{2,1,0:T(8,128)(2,1)S(1)} %all_to_all.15.own_ref), channel_id=1, source_target_pairs={{0,7},{1,6},{2,5},{3,4},{4,11},{5,10},{6,9},{7,8},{8,15},{9,14},{1... | collective-permute-start | bytes 1671176 | tf_op jit(solution)/shard_map/ppermute | solution.py:136
  37.9 5.7 %collective-permute-done.1.far_ref = bf16[4,272,256]{2,1,0:T(8,128)(2,1)S(1)} collective-permute-done((bf16[4,272,256]{2,1,0:T(8,128)(2,1)S(1)}, bf16[4,272,256]{2,1,0:T(8,128)(2,1)S(1)}, u32[]{:S(2)}, u32[]{:S(2)}) %collective-permute-start.1) | collective-permute-done | bytes 557088 | tf_op jit(solution)/shard_map/ppermute | solution.py:140
  43.6 13.3 %collective-permute-done.back_ref = bf16[4,272,256]{2,1,0:T(8,128)(2,1)S(1)} collective-permute-done((bf16[4,272,256]{2,1,0:T(8,128)(2,1)S(1)}, bf16[4,272,256]{2,1,0:T(8,128)(2,1)S(1)}, u32[]{:S(2)}, u32[]{:S(2)}) %collective-permute-start) | collective-permute-done | bytes 557088 | tf_op jit(solution)/shard_map/ppermute | solution.py:136
  56.9 0.0 all-to-all-done.1.q_ref
  56.9 0.0 copy-done.4
  56.9 8.1 %shard_map.56 = bf16[32,4,16,512]{3,2,1,0:T(8,128)(2,1)S(1)} custom-call(s32[1]{0:T(128)} %bitcast.index_ref, s32[18]{0:T(128)S(1)} %copy-done.4, bf16[4,256,512]{2,1,0:T(8,128)(2,1)S(1)} %all-to-all-done.1.q_ref, bf16[4,272,256]{2,1,0:T(8,128)(2,1)S(1)} %all_to_all.15.own_ref, bf16[4,272,256]{2,1,0:T(8,128)(2,1)S(1)} %collective-permute-done.back_ref, ...), custom_call_target="tpu_custom_call" | custom-call | tf_op jit(solution)/shard_map/pallas_call | solution.py:144
  65.0 71.9 %all_to_all.16.in_ref = bf16[32,64,512]{2,1,0:T(8,128)(2,1)S(1)} all-to-all(bf16[32,64,512]{2,1,0:T(8,128)(2,1)S(1)} %bitcast.3), channel_id=1, replica_groups=mesh['dp'=16,'ctx'=32] {'ctx'}, dimensions={0} | all-to-all | bytes 4194304 | tf_op jit(solution)/shard_map/all_to_all | solution.py:158
  136.9 1.8 %shard_map.57 = bf16[512,2048]{1,0:T(8,128)(2,1)} custom-call(bf16[32,64,512]{2,1,0:T(8,128)(2,1)S(1)} %all_to_all.16.in_ref), custom_call_target="tpu_custom_call" | custom-call | tf_op jit(solution)/shard_map/pallas_call | solution.py:161
Async XLA Ops:
  0.0 1.2 copy-start
  1.2 0.9 copy-start.1
  2.2 0.9 copy-start.2
  3.1 0.7 copy-start.3
  3.8 53.1 %copy-start.4 = (s32[18]{0:T(128)S(1)}, s32[18]{0:T(128)}, u32[]{:S(2)}) copy-start(s32[18]{0:T(128)} %doc_ref.1) | copy-start | bytes 220
  23.7 33.2 %all-to-all-start.1 = ((bf16[4,256,512]{2,1,0:T(8,128)(2,1)}), bf16[4,256,512]{2,1,0:T(8,128)(2,1)S(1)}, u32[]{:S(2)}, u32[]{:S(2)}) async-start(bf16[4,256,512]{2,1,0:T(8,128)(2,1)} %get-tuple-element.11), calls=%async_computation.1 | async-start | bytes 2097152 | tf_op jit(solution)/shard_map/all_to_all | solution.py:141
  28.7 14.9 %collective-permute-start.1 = (bf16[4,272,256]{2,1,0:T(8,128)(2,1)S(1)}, bf16[4,272,256]{2,1,0:T(8,128)(2,1)S(1)}, u32[]{:S(2)}, u32[]{:S(2)}) collective-permute-start(bf16[4,272,256]{2,1,0:T(8,128)(2,1)S(1)} %all_to_all.15.own_ref), channel_id=1, source_target_pairs={{0,8},{1,9},{2,10},{3,11},{4,12},{5,13},{6,14},{7,15},{8,16},{9,17... | collective-permute-start | bytes 1671176 | tf_op jit(solution)/shard_map/ppermute | solution.py:140
  32.2 24.7 %collective-permute-start = (bf16[4,272,256]{2,1,0:T(8,128)(2,1)S(1)}, bf16[4,272,256]{2,1,0:T(8,128)(2,1)S(1)}, u32[]{:S(2)}, u32[]{:S(2)}) collective-permute-start(bf16[4,272,256]{2,1,0:T(8,128)(2,1)S(1)} %all_to_all.15.own_ref), channel_id=1, source_target_pairs={{0,7},{1,6},{2,5},{3,4},{4,11},{5,10},{6,9},{7,8},{8,15},{9,14},{1... | collective-permute-start | bytes 1671176 | tf_op jit(solution)/shard_map/ppermute | solution.py:136

commit v4 on v2

v4 whole, which is shorter than its diff:
```python
import functools
import math

import jax
import jax.numpy as jnp
from jax import lax
from jax.experimental import pallas as pl
from jax.experimental.pallas import tpu as pltpu
from jax.sharding import PartitionSpec as P

H = 16
KVH = 4
HD = 128
GROUP = H // KVH
SPAN = 8
SCALE = math.log2(math.e) / math.sqrt(HD)


def shift(value, steps):
    count = lax.axis_size("ctx")
    return lax.ppermute(value, "ctx", [(s, (s + steps) % count) for s in range(count)])


def doc_start(doc_ref, positions):
    end = jnp.int32(0)
    start = jnp.zeros_like(positions)
    for k in range(doc_ref.shape[0]):
        end = end + doc_ref[k]
        start = jnp.where(end <= positions, end, start)
    return start


def over_group(row):
    return jnp.concatenate([row] * GROUP, axis=1)


def visit(d, base, starts, positions, q_ref, k_ref, v_ref, old, new):
    m_old, l_old, acc_old = old if d > 0 else (None, None, None)
    m_ref, l_ref, acc_ref = new
    rows = k_ref.shape[0]
    key_pos = base - d * rows + lax.broadcasted_iota(jnp.int32, (rows, rows), 0)
    visible = key_pos >= starts
    if d == 0:
        visible = visible & (key_pos <= positions)
    scores = lax.dot_general(
        k_ref[...], q_ref[0], (((1,), (0,)), ((), ())), preferred_element_type=jnp.float32
    )
    scores = jnp.where(over_group(visible), scores, -jnp.inf)
    top = jnp.max(scores, axis=0, keepdims=True)
    if d > 0:
        before = m_old[0]
        top = jnp.maximum(before, top)
    expo = jnp.exp2((scores - top) * SCALE)
    total = jnp.sum(expo, axis=0, keepdims=True)
    weighted = lax.dot_general(
        v_ref[...], expo.astype(jnp.bfloat16), (((0,), (0,)), ((), ())), preferred_element_type=jnp.float32
    )
    if d > 0:
        keep = jnp.exp2((before - top) * SCALE)
        total = l_old[0] * keep + total
        weighted = acc_old[0] * keep + weighted
    m_ref[0] = top
    l_ref[0] = total
    acc_ref[0] = weighted


def begin(devices, index_ref, doc_ref, rows_ref, k_ref, v_ref, col_ref, row_ref, m_ref, l_ref, acc_ref, q_ref, hot_ref):
    rows, slots = k_ref.shape[0], hot_ref.shape[0]
    turned = rows_ref[...].T
    q_ref[0] = jnp.concatenate([turned[g * HD : (g + 1) * HD] for g in range(GROUP)], axis=1)
    base = index_ref[0] * rows
    positions = base + lax.broadcasted_iota(jnp.int32, (1, rows), 1)
    starts = doc_start(doc_ref, positions)
    visit(0, base, starts, positions, q_ref, k_ref, v_ref, None, (m_ref, l_ref, acc_ref))

    @pl.when(pl.program_id(0) == 0)
    def _():
        earlier = lax.broadcasted_iota(jnp.int32, (rows, rows), 0) < lax.broadcasted_iota(
            jnp.int32, (rows, rows), 1
        )
        same = (col_ref[...] == row_ref[...]) & earlier
        rank = jnp.sum(same.astype(jnp.int32), axis=0, keepdims=True)
        slot = row_ref[...] * (slots // devices) + rank
        spots = lax.broadcasted_iota(jnp.int32, (slots, rows), 0)
        hot_ref[...] = (spots == slot).astype(jnp.float32).astype(jnp.bfloat16)


def proceed(dists, last, index_ref, doc_ref, q_ref, *refs):
    refs = list(refs)
    blocks = [(d, refs.pop(0), refs.pop(0)) for d in dists]
    old = refs[:3]
    if last:
        hot_ref, out_ref = refs[3:5]
        new = refs[5:]
    else:
        new = refs[3:]
    rows = q_ref.shape[2] // GROUP
    base = index_ref[0] * rows
    earliest = doc_start(doc_ref, base)

    def seen(d):
        return earliest < base - (d - 1) * rows

    def add(d, k_ref, v_ref, source):
        positions = base + lax.broadcasted_iota(jnp.int32, (1, rows), 1)
        visit(d, base, doc_start(doc_ref, positions), positions, q_ref, k_ref, v_ref, source, new)

    def end(source):
        attended = (source[2][0] / source[1][0]).astype(jnp.bfloat16)
        attended = jnp.concatenate([attended[:, g * rows : (g + 1) * rows] for g in range(GROUP)], axis=0)
        out_ref[...] = lax.dot_general(
            hot_ref[...], attended, (((1,), (1,)), ((), ())), preferred_element_type=jnp.float32
        ).astype(jnp.bfloat16)

    @pl.when(seen(dists[0]))
    def _():
        add(*blocks[0], old)
        for block in blocks[1:]:
            pl.when(seen(block[0]))(functools.partial(add, *block, new))
        if last:
            end(new)

    @pl.when(jnp.logical_not(seen(dists[0])))
    def _():
        if last:
            end(old)
        else:
            for source, target in zip(old, new):
                target[...] = source[...]


def join(k_ref, v_ref, out_ref):
    rows = k_ref.shape[0]
    out_ref[:rows] = k_ref[...]
    out_ref[rows:] = v_ref[...]


SMEM = pl.BlockSpec(memory_space=pltpu.SMEM)


def whole(shape):
    return pl.BlockSpec(shape, lambda h: (0,) * len(shape))


def per_head(*shape):
    return pl.BlockSpec((1, *shape), lambda h: (h, 0, 0))


def block_specs(rows):
    return [pl.BlockSpec((rows, HD), lambda h: (0, h)), pl.BlockSpec((rows, HD), lambda h: (1, h))]


def running(rows):
    sizes = [(1, GROUP * rows), (1, GROUP * rows), (HD, GROUP * rows)]
    return [jax.ShapeDtypeStruct((KVH, *s), jnp.float32) for s in sizes], [per_head(*s) for s in sizes]


def cost(rows, blocks):
    return pl.CostEstimate(
        flops=blocks * 4 * rows * rows * H * HD, bytes_accessed=6 << 20, transcendentals=blocks * rows * rows * H
    )


PARAMS = pltpu.CompilerParams(vmem_limit_bytes=32 << 20)


def first_step(index, doc_lengths, queries, block, row_owner, devices):
    rows = block.shape[0] // 2
    shapes, specs = running(rows)
    return pl.pallas_call(
        functools.partial(begin, devices),
        grid=(KVH,),
        in_specs=[
            SMEM, SMEM, pl.BlockSpec((rows, GROUP * HD), lambda h: (0, h)), *block_specs(rows),
            whole((rows, 1)), whole((1, rows)),
        ],
        out_specs=[*specs, per_head(HD, GROUP * rows), whole((2 * rows, rows))],
        out_shape=[
            *shapes,
            jax.ShapeDtypeStruct((KVH, HD, GROUP * rows), jnp.bfloat16),
            jax.ShapeDtypeStruct((2 * rows, rows), jnp.bfloat16),
        ],
        compiler_params=PARAMS,
        cost_estimate=cost(rows, 1),
    )(index, doc_lengths, queries, block, block, row_owner, row_owner.reshape(1, rows))


def next_step(index, doc_lengths, queries, blocks, state):
    rows = blocks[0][1].shape[0] // 2
    shapes, specs = running(rows)
    return pl.pallas_call(
        functools.partial(proceed, [d for d, _ in blocks], False),
        grid=(KVH,),
        in_specs=[SMEM, SMEM, per_head(HD, GROUP * rows), *block_specs(rows) * len(blocks), *specs],
        out_specs=specs,
        out_shape=shapes,
        compiler_params=PARAMS,
        cost_estimate=cost(rows, len(blocks)),
    )(index, doc_lengths, queries, *[b for _, block in blocks for b in (block, block)], *state)


def finish(index_ref, doc_ref, q_ref, k_ref, v_ref, m_ref, l_ref, acc_ref, hot_ref, out_ref, *scratch):
    for h in range(KVH):
        lanes = pl.ds(h * HD, HD)
        proceed(
            [SPAN // 2], True, index_ref, doc_ref, q_ref.at[pl.ds(h, 1)], k_ref.at[:, lanes], v_ref.at[:, lanes],
            *[ref.at[pl.ds(h, 1)] for ref in (m_ref, l_ref, acc_ref)], hot_ref,
            out_ref.at[:, pl.ds(h * GROUP * HD, GROUP * HD)], *scratch,
        )


def last_step(index, doc_lengths, queries, keys, values, state, hot):
    _, specs = running(keys.shape[0])
    vmem = pl.BlockSpec(memory_space=pltpu.VMEM)
    return pl.pallas_call(
        finish,
        in_specs=[SMEM, SMEM] + [vmem] * 7,
        out_specs=vmem,
        out_shape=jax.ShapeDtypeStruct((hot.shape[0], H * HD), jnp.bfloat16),
        scratch_shapes=[pltpu.VMEM(s.block_shape, jnp.float32) for s in specs],
        compiler_params=PARAMS,
        cost_estimate=cost(keys.shape[0], 1),
    )(index, doc_lengths, queries, keys, values, *state, hot)


def joined(keys, values):
    return pl.pallas_call(
        join, out_shape=jax.ShapeDtypeStruct((2 * keys.shape[0], keys.shape[1]), keys.dtype)
    )(keys, values)


def on_device(query_rows, key_rows, value_rows, doc_lengths, row_owner):
    rows, features = query_rows.shape
    devices = lax.axis_size("ctx")
    index = lax.axis_index("ctx").astype(jnp.int32).reshape(1)
    block = joined(key_rows, value_rows)
    near1, far7 = shift(block, 1), shift(block, SPAN - 1)
    *state, queries, hot = first_step(index, doc_lengths, query_rows, block, row_owner, devices)
    near1, *state = lax.optimization_barrier((near1, *state))
    near2, far6 = shift(near1, 1), shift(far7, -1)
    state = next_step(index, doc_lengths, queries, [(1, near1), (7, far7)], state)
    near2, *state = lax.optimization_barrier((near2, *state))
    near3, far5 = shift(near2, 1), shift(far6, -1)
    state = next_step(index, doc_lengths, queries, [(2, near2), (6, far6)], state)
    near3, *state = lax.optimization_barrier((near3, *state))
    k4, v4 = shift(near3[:rows], 1), shift(far5[rows:], -1)
    state = next_step(index, doc_lengths, queries, [(3, near3), (5, far5)], state)
    outgoing = last_step(index, doc_lengths, queries, k4, v4, state, hot)
    received = lax.all_to_all(
        outgoing.reshape(devices, -1, features), "ctx", split_axis=0, concat_axis=0, tiled=True
    )
    return received.reshape(-1, features)


def solution(mesh):
    rows = P(("dp", "ctx"), None)
    return jax.shard_map(
        on_device,
        mesh=mesh,
        in_specs=(rows, rows, rows, P("dp"), rows),
        out_specs=rows,
        check_vma=False,
    )
```

time: 143 us -> 135 us (0.944)
  the two profiles are of different devices: /device:TPU:200 before, /device:TPU:264 now
where the time goes in v4:
time: 135 us; the launch traced here: 133 us
  blocking collectives  58.7 us (43%)
  starting transfers between devices  31.9 us (24%)
  waiting for transfers between devices  22.1 us (16%)
  Pallas kernels  13.9 us (10%)
  local copies, waits for them, and re-layouts  5.76 us (4%)
    all_to_all x1, blocking collectives, on_device(): lax.all_to_all(outgoing.reshape(devices, -1, features), 'ctx', split_axis...  58.7 us
    ppermute x8, starting transfers between devices, shift(): lax.ppermute(value, 'ctx', [(s, (s + steps) % count) for s in range(count)])  31.9 us
    ppermute x8, waiting for transfers between devices, shift(): lax.ppermute(value, 'ctx', [(s, (s + steps) % count) for s in range(count)])  22.1 us
    pallas_call x3, Pallas kernels, next_step(): pl.pallas_call(functools.partial(proceed, [d for d, _ in blocks], False),...  6.18 us
    unnamed x12, local copies, waits for them, and re-layouts  5.73 us
    pallas_call x1, Pallas kernels, first_step(): pl.pallas_call(functools.partial(begin, devices), grid=(KVH,), in_specs=[...  3.85 us
  transfers between devices with their start and end apart: 8, of which 7 were waited for; matrix products, arithmetic and copies ran while one was open for 1% of the time, Pallas kernels for 8%

profile of v4, /device:TPU:264, one launch (start us, length us, event | category | flops | bytes accessed | tf_op | source)
XLA Modules:
  0.0 132.6 jit_solution(4725313380945701002)
XLA Ops:
  0.0 0.0 copy-start.3
  0.0 1.9 %shard_map.55.k_ref.v_ref = bf16[512,512]{1,0:T(8,128)(2,1)} custom-call(bf16[256,512]{1,0:T(8,128)(2,1)} %k_ref.1, bf16[256,512]{1,0:T(8,128)(2,1)} %v_ref.1), custom_call_target="tpu_custom_call" | custom-call | tf_op jit(solution)/shard_map/pallas_call | solution.py:227
  1.9 3.5 %collective-permute-start = (bf16[512,512]{1,0:T(8,128)(2,1)}, bf16[512,512]{1,0:T(8,128)(2,1)S(1)}, u32[]{:S(2)}, u32[]{:S(2)}) collective-permute-start(bf16[512,512]{1,0:T(8,128)(2,1)} %shard_map.55.k_ref.v_ref), channel_id=1, source_target_pairs={{0,1},{1,2},{2,3},{3,4},{4,5},{5,6},{6,7},{7,8},{8,9},{9,10},{10,1... | collective-permute-start | bytes 1572872 | tf_op jit(solution)/shard_map/ppermute | solution.py:21
  5.4 3.3 %collective-permute-start.2 = (bf16[512,512]{1,0:T(8,128)(2,1)}, bf16[512,512]{1,0:T(8,128)(2,1)S(1)}, u32[]{:S(2)}, u32[]{:S(2)}) collective-permute-start(bf16[512,512]{1,0:T(8,128)(2,1)} %shard_map.55.k_ref.v_ref), channel_id=1, source_target_pairs={{0,7},{1,8},{2,9},{3,10},{4,11},{5,12},{6,13},{7,14},{8,15},{9,16}... | collective-permute-start | bytes 1572872 | tf_op jit(solution)/shard_map/ppermute | solution.py:21
  8.6 0.8 copy.6.col_ref
  9.5 0.0 copy-start
  9.5 1.0 copy-done
  10.5 1.2 copy-done.1
  11.7 0.7 copy-done.2
  12.4 0.7 copy-done.4
  13.1 3.8 %shard_map.56 = (f32[4,1,1024]{2,1,0:T(1,128)S(1)}, f32[4,1,1024]{2,1,0:T(1,128)S(1)}, f32[4,128,1024]{2,1,0:T(8,128)S(1)}, bf16[4,128,1024]{2,1,0:T(8,128)(2,1)S(1)}, bf16[512,256]{1,0:T(8,128)(2,1)S(1)}) custom-call(s32[1]{0:T(128)} %bitcast.index_ref, s32[18]{0:T(128)S(1)} %copy-done.2, bf16[256,2048]{1,0:T(8,128)(2,1)S(1)} %copy-done.1, ...), custom_call_target="tpu_custom_call" | custom-call | flops 536870912 | bytes 6291456 | tf_op jit(solution)/shard_map/pallas_call | solution.py:170
  16.9 0.7 collective-permute-done.refs_0_.refs_1_
  17.6 3.5 %collective-permute-start.1 = (bf16[512,512]{1,0:T(8,128)(2,1)S(1)}, bf16[512,512]{1,0:T(8,128)(2,1)S(1)}, u32[]{:S(2)}, u32[]{:S(2)}) collective-permute-start(bf16[512,512]{1,0:T(8,128)(2,1)S(1)} %collective-permute-done.refs_0_.refs_1_), channel_id=1, source_target_pairs={{0,1},{1,2},{2,3},{3,4},{4,5},{5,6},{6,7},{7,8},{8,9},{9,10},{10,1... | collective-permute-start | bytes 1572872 | tf_op jit(solution)/shard_map/ppermute | solution.py:21
  21.1 7.9 %collective-permute-done.2.refs_2_.refs_3_ = bf16[512,512]{1,0:T(8,128)(2,1)S(1)} collective-permute-done((bf16[512,512]{1,0:T(8,128)(2,1)}, bf16[512,512]{1,0:T(8,128)(2,1)S(1)}, u32[]{:S(2)}, u32[]{:S(2)}) %collective-permute-start.2) | collective-permute-done | bytes 524320 | tf_op jit(solution)/shard_map/ppermute | solution.py:21
  29.0 6.1 %collective-permute-start.4 = (bf16[512,512]{1,0:T(8,128)(2,1)S(1)}, bf16[512,512]{1,0:T(8,128)(2,1)S(1)}, u32[]{:S(2)}, u32[]{:S(2)}) collective-permute-start(bf16[512,512]{1,0:T(8,128)(2,1)S(1)} %collective-permute-done.2.refs_2_.refs_3_), channel_id=1, source_target_pairs={{0,31},{1,0},{2,1},{3,2},{4,3},{5,4},{6,5},{7,6},{8,7},{9,8},{10,9... | collective-permute-start | bytes 1572872 | tf_op jit(solution)/shard_map/ppermute | solution.py:21
  35.1 0.0 copy-done.3
  35.2 3.9 %shard_map.57 = (f32[4,1,1024]{2,1,0:T(1,128)S(1)}, f32[4,1,1024]{2,1,0:T(1,128)S(1)}, f32[4,128,1024]{2,1,0:T(8,128)S(1)}) custom-call(s32[1]{0:T(128)} %bitcast.index_ref, s32[18]{0:T(128)S(1)} %copy-done.3, bf16[4,128,1024]{2,1,0:T(8,128)(2,1)S(1)} %get-tuple-element.31.q_ref, bf16[512,512]{1,0:T(8,128)(2,1)S(1)} %collective-permute-done.refs_0_.refs_1_, ...), custom_call_target="tpu_custom_call" | custom-call | flops 1073741824 | bytes 6291456 | tf_op jit(solution)/shard_map/pallas_call | solution.py:191
  39.0 2.1 %collective-permute-done.1.refs_0_.refs_1_ = bf16[512,512]{1,0:T(8,128)(2,1)S(1)} collective-permute-done((bf16[512,512]{1,0:T(8,128)(2,1)S(1)}, bf16[512,512]{1,0:T(8,128)(2,1)S(1)}, u32[]{:S(2)}, u32[]{:S(2)}) %collective-permute-start.1) | collective-permute-done | bytes 524320 | tf_op jit(solution)/shard_map/ppermute | solution.py:21
  41.2 1.9 %collective-permute-start.3 = (bf16[512,512]{1,0:T(8,128)(2,1)S(1)}, bf16[512,512]{1,0:T(8,128)(2,1)S(1)}, u32[]{:S(2)}, u32[]{:S(2)}) collective-permute-start(bf16[512,512]{1,0:T(8,128)(2,1)S(1)} %collective-permute-done.1.refs_0_.refs_1_), channel_id=1, source_target_pairs={{0,1},{1,2},{2,3},{3,4},{4,5},{5,6},{6,7},{7,8},{8,9},{9,10},{10,1... | collective-permute-start | bytes 1572872 | tf_op jit(solution)/shard_map/ppermute | solution.py:21
  43.1 2.2 %collective-permute-done.4.refs_2_.refs_3_ = bf16[512,512]{1,0:T(8,128)(2,1)S(1)} collective-permute-done((bf16[512,512]{1,0:T(8,128)(2,1)S(1)}, bf16[512,512]{1,0:T(8,128)(2,1)S(1)}, u32[]{:S(2)}, u32[]{:S(2)}) %collective-permute-start.4) | collective-permute-done | bytes 524320 | tf_op jit(solution)/shard_map/ppermute | solution.py:21
  45.3 4.8 %collective-permute-start.6 = (bf16[512,512]{1,0:T(8,128)(2,1)S(1)}, bf16[512,512]{1,0:T(8,128)(2,1)S(1)}, u32[]{:S(2)}, u32[]{:S(2)}) collective-permute-start(bf16[512,512]{1,0:T(8,128)(2,1)S(1)} %collective-permute-done.4.refs_2_.refs_3_), channel_id=1, source_target_pairs={{0,31},{1,0},{2,1},{3,2},{4,3},{5,4},{6,5},{7,6},{8,7},{9,8},{10,9... | collective-permute-start | bytes 1572872 | tf_op jit(solution)/shard_map/ppermute | solution.py:21
  50.1 1.1 shard_map.58
  51.2 6.5 %collective-permute-done.3.refs_0_.refs_1_ = bf16[512,512]{1,0:T(8,128)(2,1)S(1)} collective-permute-done((bf16[512,512]{1,0:T(8,128)(2,1)S(1)}, bf16[512,512]{1,0:T(8,128)(2,1)S(1)}, u32[]{:S(2)}, u32[]{:S(2)}) %collective-permute-start.3) | collective-permute-done | bytes 524320 | tf_op jit(solution)/shard_map/ppermute | solution.py:21
  57.7 1.9 %collective-permute-start.5 = (bf16[256,512]{1,0:T(8,128)(2,1)S(1)}, bf16[256,512]{1,0:T(8,128)(2,1)S(1)}, u32[]{:S(2)}, u32[]{:S(2)}) collective-permute-start(bf16[256,512]{1,0:T(8,128)(2,1)S(1)} %slice.6), channel_id=1, source_target_pairs={{0,1},{1,2},{2,3},{3,4},{4,5},{5,6},{6,7},{7,8},{8,9},{9,10},{10,1... | collective-permute-start | bytes 786440 | tf_op jit(solution)/shard_map/ppermute | solution.py:21
  59.7 0.0 collective-permute-done.6.refs_2_.refs_3_
  59.7 7.0 %collective-permute-start.7 = (bf16[256,512]{1,0:T(8,128)(2,1)S(1)}, bf16[256,512]{1,0:T(8,128)(2,1)S(1)}, u32[]{:S(2)}, u32[]{:S(2)}) collective-permute-start(bf16[256,512]{1,0:T(8,128)(2,1)S(1)} %slice.8), channel_id=1, source_target_pairs={{0,31},{1,0},{2,1},{3,2},{4,3},{5,4},{6,5},{7,6},{8,7},{9,8},{10,9... | collective-permute-start | bytes 786440 | tf_op jit(solution)/shard_map/ppermute | solution.py:21
  66.7 1.1 shard_map.59
  67.8 1.2 collective-permute-done.5.k_ref
  69.0 1.5 %collective-permute-done.7.v_ref = bf16[256,512]{1,0:T(8,128)(2,1)S(1)} collective-permute-done((bf16[256,512]{1,0:T(8,128)(2,1)S(1)}, bf16[256,512]{1,0:T(8,128)(2,1)S(1)}, u32[]{:S(2)}, u32[]{:S(2)}) %collective-permute-start.7) | collective-permute-done | bytes 262176 | tf_op jit(solution)/shard_map/ppermute | solution.py:21
  70.5 2.0 %shard_map.60 = bf16[512,2048]{1,0:T(8,128)(2,1)S(1)} custom-call(s32[1]{0:T(128)} %bitcast.index_ref, s32[18]{0:T(128)S(1)} %copy-done.3, bf16[4,128,1024]{2,1,0:T(8,128)(2,1)S(1)} %get-tuple-element.31.q_ref, bf16[256,512]{1,0:T(8,128)(2,1)S(1)} %collective-permute-done.5.k_ref, bf16[256,512]{1,0:T(8,128)(2,1)S(1)} %collective-permute-done.7.v_ref, ...), custom_call_target="tpu_custom_call" | custom-call | flops 536870912 | bytes 6291456 | tf_op jit(solution)/shard_map/pallas_call | solution.py:215
  72.5 58.7 %all_to_all.5 = bf16[32,16,2048]{2,1,0:T(8,128)(2,1)S(1)} all-to-all(bf16[32,16,2048]{2,1,0:T(8,128)(2,1)S(1)} %bitcast.4), channel_id=1, replica_groups=mesh['dp'=16,'ctx'=32] {'ctx'}, dimensions={0} | all-to-all | bytes 4194304 | tf_op jit(solution)/shard_map/all_to_all | solution.py:249
  131.3 1.3 copy.8
  (5 shorter events, 0.0 us)
Async XLA Ops:
  0.0 35.1 %copy-start.3 = (s32[18]{0:T(128)S(1)}, s32[18]{0:T(128)}, u32[]{:S(2)}) copy-start(s32[18]{0:T(128)} %doc_ref.9) | copy-start | bytes 220
  1.9 15.8 %collective-permute-start = (bf16[512,512]{1,0:T(8,128)(2,1)}, bf16[512,512]{1,0:T(8,128)(2,1)S(1)}, u32[]{:S(2)}, u32[]{:S(2)}) collective-permute-start(bf16[512,512]{1,0:T(8,128)(2,1)} %shard_map.55.k_ref.v_ref), channel_id=1, source_target_pairs={{0,1},{1,2},{2,3},{3,4},{4,5},{5,6},{6,7},{7,8},{8,9},{9,10},{10,1... | collective-permute-start | bytes 1572872 | tf_op jit(solution)/shard_map/ppermute | solution.py:21
  5.4 23.7 %collective-permute-start.2 = (bf16[512,512]{1,0:T(8,128)(2,1)}, bf16[512,512]{1,0:T(8,128)(2,1)S(1)}, u32[]{:S(2)}, u32[]{:S(2)}) collective-permute-start(bf16[512,512]{1,0:T(8,128)(2,1)} %shard_map.55.k_ref.v_ref), channel_id=1, source_target_pairs={{0,7},{1,8},{2,9},{3,10},{4,11},{5,12},{6,13},{7,14},{8,15},{9,16}... | collective-permute-start | bytes 1572872 | tf_op jit(solution)/shard_map/ppermute | solution.py:21
  9.5 1.0 copy-start
  10.5 1.2 copy-start.1
  11.7 0.7 copy-start.2
  12.4 0.7 copy-start.4
  17.6 23.6 %collective-permute-start.1 = (bf16[512,512]{1,0:T(8,128)(2,1)S(1)}, bf16[512,512]{1,0:T(8,128)(2,1)S(1)}, u32[]{:S(2)}, u32[]{:S(2)}) collective-permute-start(bf16[512,512]{1,0:T(8,128)(2,1)S(1)} %collective-permute-done.refs_0_.refs_1_), channel_id=1, source_target_pairs={{0,1},{1,2},{2,3},{3,4},{4,5},{5,6},{6,7},{7,8},{8,9},{9,10},{10,1... | collective-permute-start | bytes 1572872 | tf_op jit(solution)/shard_map/ppermute | solution.py:21
  29.0 16.2 %collective-permute-start.4 = (bf16[512,512]{1,0:T(8,128)(2,1)S(1)}, bf16[512,512]{1,0:T(8,128)(2,1)S(1)}, u32[]{:S(2)}, u32[]{:S(2)}) collective-permute-start(bf16[512,512]{1,0:T(8,128)(2,1)S(1)} %collective-permute-done.2.refs_2_.refs_3_), channel_id=1, source_target_pairs={{0,31},{1,0},{2,1},{3,2},{4,3},{5,4},{6,5},{7,6},{8,7},{9,8},{10,9... | collective-permute-start | bytes 1572872 | tf_op jit(solution)/shard_map/ppermute | solution.py:21
  41.2 16.5 %collective-permute-start.3 = (bf16[512,512]{1,0:T(8,128)(2,1)S(1)}, bf16[512,512]{1,0:T(8,128)(2,1)S(1)}, u32[]{:S(2)}, u32[]{:S(2)}) collective-permute-start(bf16[512,512]{1,0:T(8,128)(2,1)S(1)} %collective-permute-done.1.refs_0_.refs_1_), channel_id=1, source_target_pairs={{0,1},{1,2},{2,3},{3,4},{4,5},{5,6},{6,7},{7,8},{8,9},{9,10},{10,1... | collective-permute-start | bytes 1572872 | tf_op jit(solution)/shard_map/ppermute | solution.py:21
  45.3 14.4 %collective-permute-start.6 = (bf16[512,512]{1,0:T(8,128)(2,1)S(1)}, bf16[512,512]{1,0:T(8,128)(2,1)S(1)}, u32[]{:S(2)}, u32[]{:S(2)}) collective-permute-start(bf16[512,512]{1,0:T(8,128)(2,1)S(1)} %collective-permute-done.4.refs_2_.refs_3_), channel_id=1, source_target_pairs={{0,31},{1,0},{2,1},{3,2},{4,3},{5,4},{6,5},{7,6},{8,7},{9,8},{10,9... | collective-permute-start | bytes 1572872 | tf_op jit(solution)/shard_map/ppermute | solution.py:21
  57.7 11.3 %collective-permute-start.5 = (bf16[256,512]{1,0:T(8,128)(2,1)S(1)}, bf16[256,512]{1,0:T(8,128)(2,1)S(1)}, u32[]{:S(2)}, u32[]{:S(2)}) collective-permute-start(bf16[256,512]{1,0:T(8,128)(2,1)S(1)} %slice.6), channel_id=1, source_target_pairs={{0,1},{1,2},{2,3},{3,4},{4,5},{5,6},{6,7},{7,8},{8,9},{9,10},{10,1... | collective-permute-start | bytes 786440 | tf_op jit(solution)/shard_map/ppermute | solution.py:21
  59.7 10.8 %collective-permute-start.7 = (bf16[256,512]{1,0:T(8,128)(2,1)S(1)}, bf16[256,512]{1,0:T(8,128)(2,1)S(1)}, u32[]{:S(2)}, u32[]{:S(2)}) collective-permute-start(bf16[256,512]{1,0:T(8,128)(2,1)S(1)} %slice.8), channel_id=1, source_target_pairs={{0,31},{1,0},{2,1},{3,2},{4,3},{5,4},{6,5},{7,6},{8,7},{9,8},{10,9... | collective-permute-start | bytes 786440 | tf_op jit(solution)/shard_map/ppermute | solution.py:21
